TPU v7x, 256 devices: a whole 4x4x8 slice. The times are simulated.
256 devices in a mesh: dp: 16 (over z, core), fsdp: 16 (over y, x).
Axes of the slice: x: 4, y: 4, z: 8, core: 2. Of those that a mesh axis runs over, the one named last changes fastest.
Arguments:
- hidden: bfloat16 [65536, 8192], P(('dp', 'fsdp')), may hold values from -8 to 8
- gain: float32 [8192], replicated, may hold values from 0.1 to 1.9
- qkv_weight: bfloat16 [8192, 1280], P('fsdp'), may hold values from -4 to 4
- owner_segment: int32 [65536], P(('dp', 'fsdp')), may hold values from 0 to 15, as said below
- target_row: int32 [65536], P(('dp', 'fsdp')), may hold values from 0 to 65535, as said below
Outputs:
- context: bfloat16 [65536, 1024], P(('dp', 'fsdp'))
Inputs may be any that keep to these rules, and one draw needn't show every extreme that they name: `owner_segment`: rows of one device with equal values form one sequence, and the values never fall along a device's rows. `target_row`: A permutation of the rows. A row goes to a device of the same fsdp index; a sequence's rows land on consecutive rows of one device, in order; at most 32 rows of one device go to one device, and some device sends exactly 32 to one in every draw.
All inputs are finite; a program needn't handle non-finite values.
Results may differ from a plain program's by a relative error of at most 0.012.
The roundings to bfloat16 on the way count: a program that leaves them out, or rounds other values in their place, can miss the bound.
Values may be sent and summed in bfloat16 or wider, within the bound.
A program may use at most 128 MiB of HBM per device.

v0:
```python
import jax
import jax.numpy as jnp
from jax import lax
from jax.sharding import PartitionSpec as P

HEAD = 128
GROUP = 8


EPS = 1e-05


def attend(projected, segment, position):
    count = projected.shape[0]
    query = projected[:, : GROUP * HEAD].reshape(count, GROUP, HEAD)
    keys = projected[:, GROUP * HEAD : (GROUP + 1) * HEAD]
    values = projected[:, (GROUP + 1) * HEAD :]
    scores = jnp.einsum("qgh,kh->gqk", query, keys, preferred_element_type=jnp.float32) * HEAD ** (
        -0.5
    )
    allowed = (segment[:, None] == segment[None, :]) & (position[None, :] <= position[:, None])
    scores = jnp.where(allowed[None], scores, -1e30)
    peak = jnp.max(scores, axis=2, keepdims=True)
    expos = jnp.exp(scores - peak)
    weights = (expos / jnp.sum(expos, axis=2, keepdims=True)).astype(jnp.bfloat16)
    context = jnp.einsum("gqk,kh->qgh", weights, values, preferred_element_type=jnp.float32)
    return context.reshape(count, GROUP * HEAD).astype(jnp.bfloat16)


def per_device(hidden, gain, qkv_weight, owner_segment, target_row):
    count = hidden.shape[0]
    floats = hidden.astype(jnp.float32)
    normed = (
        floats * lax.rsqrt(jnp.mean(floats * floats, axis=1, keepdims=True) + EPS) * gain
    ).astype(jnp.bfloat16)
    summed = jnp.dot(
        normed,
        lax.all_gather(qkv_weight, "fsdp", axis=0, tiled=True),
        preferred_element_type=jnp.float32,
    )
    projected = summed.astype(jnp.bfloat16)
    dp_size = lax.axis_size("dp")
    fsdp_size = lax.axis_size("fsdp")
    capacity = 2 * count // dp_size
    target_shard = target_row // count // fsdp_size
    target_slot = target_row % count
    onehot = (target_shard[:, None] == jnp.arange(dp_size, dtype=jnp.int32)[None, :]).astype(
        jnp.int32
    )
    before = jnp.cumsum(onehot, axis=0) - onehot
    bucket = target_shard * capacity + jnp.sum(before * onehot, axis=1)
    position = jnp.arange(count, dtype=jnp.int32)

    def pack_ints(entries, filler):
        buffer = jnp.full((dp_size * capacity,), filler, jnp.int32).at[bucket].set(entries)
        return buffer.reshape(dp_size, capacity)

    def place(received, arrived):
        flat = received.reshape((dp_size * capacity,) + received.shape[2:])
        return (
            jnp.zeros((count,) + flat.shape[1:], flat.dtype)
            .at[arrived.reshape(-1)]
            .set(flat, mode="drop")
        )

    slots = pack_ints(target_slot, count)
    seg_key = lax.axis_index("dp") * dp_size + owner_segment
    buffer = (
        jnp.zeros((dp_size * capacity, projected.shape[1]), projected.dtype)
        .at[bucket]
        .set(projected)
    )
    payload = lax.all_to_all(
        buffer.reshape(dp_size, capacity, projected.shape[1]),
        "dp",
        split_axis=0,
        concat_axis=0,
        tiled=True,
    )
    arrived = lax.all_to_all(slots, "dp", split_axis=0, concat_axis=0, tiled=True)
    seg_arrived = lax.all_to_all(
        pack_ints(seg_key, 0), "dp", split_axis=0, concat_axis=0, tiled=True
    )
    pos_arrived = lax.all_to_all(
        pack_ints(position, 0), "dp", split_axis=0, concat_axis=0, tiled=True
    )
    trainer_rows = place(payload, arrived)
    trainer_segment = place(seg_arrived, arrived)
    trainer_position = place(pos_arrived, arrived)
    result = attend(trainer_rows, trainer_segment, trainer_position)
    return result


def solution(mesh):
    in_specs = (P(("dp", "fsdp"), None), P(), P("fsdp", None), P(("dp", "fsdp")), P(("dp", "fsdp")))
    out_specs = P(("dp", "fsdp"), None)
    return jax.shard_map(
        per_device, mesh=mesh, in_specs=in_specs, out_specs=out_specs, check_vma=False
    )
```

profile of v0, /device:TPU:1, one launch (start us, length us, event | category | flops | bytes accessed | tf_op | source)
XLA Modules:
  0.0 221.7 jit_solution(13825894919945252709)
XLA Ops:
  6.5 0.0 all-gather.2.cloned.1.call-start
  6.5 0.7 all-gather.2.cloned.1.call-update
  7.3 0.7 and_select_fusion
  8.0 0.6 reduce-window.6
  8.6 0.2 slice_reduce_fusion
  8.8 0.1 fusion.24
  8.9 0.7 broadcast_add_fusion
  9.6 1.4 scatter_custom_fusion.3
  11.0 0.7 all_to_all.24
  11.7 10.0 %all-to-all-start.2 = ((s32[16,1,32]{2,1,0:T(1,128)}), s32[16,1,32]{2,1,0:T(1,128)S(1)}, u32[]{:S(2)}, u32[]{:S(2)}) async-start(s32[16,1,32]{2,1,0:T(1,128)} %all_to_all.24), calls=%async_computation.2 | async-start | bytes 16384 | tf_op jit(solution)/shard_map/all_to_all | solution.py:81
  21.6 0.0 copy-start
  21.6 3.1 %fusion.1 = f32[256]{0:T(256)S(1)} fusion(bf16[256,8192]{1,0:T(8,128)(2,1)} %param.5), kind=kLoop, calls=%fused_computation.10 | loop fusion | flops 6291200 | bytes 4195328 | tf_op jit(solution)/shard_map/reduce_sum | solution.py:34
  24.8 1.4 scatter_custom_fusion
  26.2 0.7 all_to_all.21
  26.8 1.8 all-to-all-done.2
  28.7 5.4 %all-to-all-start = ((s32[16,1,32]{2,1,0:T(1,128)}), s32[16,1,32]{2,1,0:T(1,128)S(1)}, u32[]{:S(2)}, u32[]{:S(2)}) async-start(s32[16,1,32]{2,1,0:T(1,128)} %all_to_all.21), calls=%async_computation | async-start | bytes 16384 | tf_op jit(solution)/shard_map/all_to_all | solution.py:80
  34.1 1.4 scatter_custom_fusion.5
  35.5 0.7 all_to_all.26
  36.2 4.8 %all-to-all-done = s32[16,1,32]{2,1,0:T(1,128)S(1)} async-done(((s32[16,1,32]{2,1,0:T(1,128)}), s32[16,1,32]{2,1,0:T(1,128)S(1)}, u32[]{:S(2)}, u32[]{:S(2)}) %all-to-all-start) | async-done | bytes 2080 | tf_op jit(solution)/shard_map/all_to_all | solution.py:80
  41.0 3.9 %all-to-all-start.3 = ((s32[16,1,32]{2,1,0:T(1,128)}), s32[16,1,32]{2,1,0:T(1,128)S(1)}, u32[]{:S(2)}, u32[]{:S(2)}) async-start(s32[16,1,32]{2,1,0:T(1,128)} %all_to_all.26), calls=%async_computation.3 | async-start | bytes 16384 | tf_op jit(solution)/shard_map/all_to_all | solution.py:84
  44.9 106.5 %all-gather.2.cloned.1.call-done = bf16[8192,1280]{1,0:T(8,128)(2,1)} async-done(((bf16[512,1280]{1,0:T(8,128)(2,1)}), bf16[8192,1280]{1,0:T(8,128)(2,1)}) %all-gather.2.cloned.1.call-update) | async-done | bytes 20971536 | tf_op jit(solution)/shard_map/all_gather | solution.py:38
  151.4 0.0 copy-done
  151.4 13.6 %fusion.8 = bf16[256,1280]{1,0:T(8,128)(2,1)S(1)} fusion(bf16[8192,1280]{1,0:T(8,128)(2,1)} %all-gather.2.cloned.1.call-done, bf16[256,8192]{1,0:T(8,128)(2,1)} %param.5, f32[8192]{0:T(1024)S(1)} %copy-done, f32[256]{0:T(256)S(1)} %add_rsqrt_fusion), kind=kOutput, calls=%fused_computation.16 | convolution fusion | flops 5377425408 | bytes 25854976 | tf_op jit(solution)/shard_map/dot_general | solution.py:36
  165.0 2.9 %scatter_custom_fusion.1 = bf16[512,1280]{1,0:T(8,128)(2,1)} fusion(s32[256]{0:T(256)S(1)} %compare_select_fusion.1, bf16[256,1280]{1,0:T(8,128)(2,1)S(1)} %fusion.8, bf16[]{:T(256)} %constant.53.clone.1), kind=kCustom, calls=%fused_computation.25 | custom fusion | bytes 1310722 | tf_op jit(solution)/shard_map/scatter | solution.py:71
  167.9 0.0 all-to-all-done.3
  167.9 7.7 %all-to-all-start.1 = ((bf16[16,32,1280]{2,1,0:T(8,128)(2,1)}), bf16[16,32,1280]{2,1,0:T(8,128)(2,1)S(1)}, u32[]{:S(2)}, u32[]{:S(2)}) async-start(bf16[16,32,1280]{2,1,0:T(8,128)(2,1)} %bitcast.3), calls=%async_computation.1 | async-start | bytes 2621440 | tf_op jit(solution)/shard_map/all_to_all | solution.py:73
  175.6 0.5 broadcast.169
  176.1 0.7 reduce.13
  176.8 0.1 reshape.190
  176.9 0.7 reduce.11
  177.5 0.1 reshape.148
  177.6 0.7 reduce.12
  178.3 0.1 reshape.206
  178.4 2.6 %scatter_custom_fusion.4 = s32[256]{0:T(256)S(1)} fusion(s32[512]{0:T(512)S(1)} %bitcast.69, s32[512]{0:T(512)S(1)} %reshape.190, s32[]{:T(128)} %constant.56.clone.1), kind=kCustom, calls=%fused_computation.63 | custom fusion | bytes 1028 | tf_op jit(solution)/shard_map/scatter | solution.py:63
  181.0 2.4 %scatter_custom_fusion.6 = s32[256]{0:T(256)S(1)} fusion(s32[512]{0:T(512)S(1)} %bitcast.70, s32[512]{0:T(512)S(1)} %reshape.206, s32[]{:T(128)} %constant.56.clone.1), kind=kCustom, calls=%fused_computation.65 | custom fusion | bytes 1028 | tf_op jit(solution)/shard_map/scatter | solution.py:63
  183.4 0.1 compare_and_fusion
  183.6 25.2 %all-to-all-done.1 = bf16[16,32,1280]{2,1,0:T(8,128)(2,1)S(1)} async-done(((bf16[16,32,1280]{2,1,0:T(8,128)(2,1)}), bf16[16,32,1280]{2,1,0:T(8,128)(2,1)S(1)}, u32[]{:S(2)}, u32[]{:S(2)}) %all-to-all-start.1) | async-done | bytes 1310752 | tf_op jit(solution)/shard_map/all_to_all | solution.py:73
  208.8 2.9 %scatter_custom_fusion.2 = bf16[256,1280]{1,0:T(8,128)(2,1)S(1)} fusion(s32[512]{0:T(512)S(1)} %bitcast.71, bf16[512,1280]{1,0:T(8,128)(2,1)S(1)} %bitcast.64, bf16[]{:T(256)} %constant.53.clone.1), kind=kCustom, calls=%fused_computation.27 | custom fusion | bytes 655362 | tf_op jit(solution)/shard_map/scatter | solution.py:63
  211.7 0.1 slice.23
  211.7 0.2 copy.10
  211.9 0.8 fusion.43
  212.7 1.1 convolution_convert_fusion
  213.8 1.0 copy.14
  (7 shorter events, 0.1 us)
Async XLA Ops:
  6.5 144.8 %all-gather.2.cloned.1.call-start = ((), (), s32[]{:S(2)}) async-start(), calls=%async_computation.4 | async-start | bytes 22282240 | tf_op jit(solution)/shard_map/all_gather | solution.py:38
  11.7 17.0 %all-to-all-start.2 = ((s32[16,1,32]{2,1,0:T(1,128)}), s32[16,1,32]{2,1,0:T(1,128)S(1)}, u32[]{:S(2)}, u32[]{:S(2)}) async-start(s32[16,1,32]{2,1,0:T(1,128)} %all_to_all.24), calls=%async_computation.2 | async-start | bytes 16384 | tf_op jit(solution)/shard_map/all_to_all | solution.py:81
  21.6 129.7 %copy-start = (f32[8192]{0:T(1024)S(1)}, f32[8192]{0:T(1024)}, u32[]{:S(2)}) copy-start(f32[8192]{0:T(1024)} %param.6) | copy-start | bytes 98308
  28.7 12.4 %all-to-all-start = ((s32[16,1,32]{2,1,0:T(1,128)}), s32[16,1,32]{2,1,0:T(1,128)S(1)}, u32[]{:S(2)}, u32[]{:S(2)}) async-start(s32[16,1,32]{2,1,0:T(1,128)} %all_to_all.21), calls=%async_computation | async-start | bytes 16384 | tf_op jit(solution)/shard_map/all_to_all | solution.py:80
  41.0 126.9 %all-to-all-start.3 = ((s32[16,1,32]{2,1,0:T(1,128)}), s32[16,1,32]{2,1,0:T(1,128)S(1)}, u32[]{:S(2)}, u32[]{:S(2)}) async-start(s32[16,1,32]{2,1,0:T(1,128)} %all_to_all.26), calls=%async_computation.3 | async-start | bytes 16384 | tf_op jit(solution)/shard_map/all_to_all | solution.py:84
  167.9 40.9 %all-to-all-start.1 = ((bf16[16,32,1280]{2,1,0:T(8,128)(2,1)}), bf16[16,32,1280]{2,1,0:T(8,128)(2,1)S(1)}, u32[]{:S(2)}, u32[]{:S(2)}) async-start(bf16[16,32,1280]{2,1,0:T(8,128)(2,1)} %bitcast.3), calls=%async_computation.1 | async-start | bytes 2621440 | tf_op jit(solution)/shard_map/all_to_all | solution.py:73
Sparse Core Ops, SparseCore 0:
  9.8 141.5 all-gather.1
where the time goes:
time: 222 us
  waiting for transfers between devices  139 us (63%)
  starting transfers between devices  27 us (12%)
  local copies, waits for them, and re-layouts  19.2 us (9%)
  matrix products  15.5 us (7%)
  between operations  13.5 us (6%)
  other arithmetic  7.38 us (3%)
    all_gather x1, waiting for transfers between devices, per_device(): lax.all_gather(qkv_weight, 'fsdp', axis=0, tiled=True)  106 us
    all_to_all x1, waiting for transfers between devices, per_device(): lax.all_to_all(buffer.reshape(dp_size, capacity, projected.shape[1]), 'dp...  25.2 us
    dot_general x1, matrix products, per_device(): jnp.dot(normed, lax.all_gather(qkv_weight, 'fsdp', axis=0, tiled=True), p...  13.6 us
    all_to_all x1, starting transfers between devices, per_device(): lax.all_to_all(pack_ints(seg_key, 0), 'dp', split_axis=0, concat_axis=0,...  9.98 us
    scatter x3, local copies, waits for them, and re-layouts, place(): return jnp.zeros((count,) + flat.shape[1:], flat.dtype).at[arrived.reshap...  7.91 us
    all_to_all x1, starting transfers between devices, per_device(): lax.all_to_all(buffer.reshape(dp_size, capacity, projected.shape[1]), 'dp...  7.7 us
    all_to_all x1, starting transfers between devices, per_device(): lax.all_to_all(slots, 'dp', split_axis=0, concat_axis=0, tiled=True)  5.41 us
    all_to_all x1, waiting for transfers between devices, per_device(): lax.all_to_all(slots, 'dp', split_axis=0, concat_axis=0, tiled=True)  4.85 us
  transfers between devices with their start and end apart: 5, of which 4 were waited for; matrix products, arithmetic and copies ran while one was open for 15% of the time, Pallas kernels for 0%

commit v1 on v0

v1 whole, which is shorter than its diff:
```python
import jax
import jax.numpy as jnp
from jax import lax
from jax.experimental import pallas as pl
from jax.experimental.pallas import tpu as pltpu
from jax.sharding import PartitionSpec as P

MESH = pl.DeviceIdType.MESH
HEAD = 128
EPS = 1e-05
ROWS = 256
FEATURES = 8192
PEERS = 16
CAPACITY = 32
WIDTH = 256
STARTS = (1024, 0, 256, 512, 768)
CHUNKS = len(STARTS)
QUERIES = CHUNKS - 1


def nt(a, b):
    return lax.dot_general(a, b, (((1,), (1,)), ((), ())), preferred_element_type=jnp.float32)


def nn(a, b):
    return jnp.dot(a, b, preferred_element_type=jnp.float32)


def kernel(
    hidden, gain, weight, segment, target, out,
    gathered, normed, total, keys, values, mask, spread, collect,
    outgoing, incoming, slots_out, slots_in,
    local_sem, g_send, g_recv, a_send, a_recv, s_send, s_recv,
):
    dp, fsdp = lax.axis_index("dp"), lax.axis_index("fsdp")
    core = lax.rem(dp, 2)
    y, x = fsdp // 4, lax.rem(fsdp, 4)
    x_up, x_down, x_far = lax.rem(x + 1, 4), lax.rem(x + 3, 4), lax.rem(x + 2, 4)
    y_up, y_down, y_far = lax.rem(y + 1, 4), lax.rem(y + 3, 4), lax.rem(y + 2, 4)
    to_x_up, to_x_down = (dp, y * 4 + x_up), (dp, y * 4 + x_down)
    to_y_up, to_y_down = (dp, y_up * 4 + x), (dp, y_down * 4 + x)
    sibling = (dp + 1 - 2 * core, fsdp)

    barrier = pltpu.get_barrier_semaphore()
    for neighbour in (to_x_up, to_x_down, to_y_up, to_y_down):
        pl.semaphore_signal(barrier, inc=1, device_id=neighbour, device_id_type=MESH)

    def greet(k, carry):
        peer = (lax.rem(dp + k, PEERS), fsdp)
        pl.semaphore_signal(barrier, inc=1, device_id=peer, device_id_type=MESH)
        return carry

    lax.fori_loop(1, PEERS, greet, 0)

    own = [
        pltpu.make_async_copy(
            weight.at[core, :, :, pl.ds(STARTS[j], WIDTH)],
            gathered.at[j, y, x, core],
            local_sem.at[j],
        )
        for j in range(CHUNKS)
    ]
    for copy in own:
        copy.start()
    load = pltpu.make_async_copy(hidden, normed, local_sem.at[CHUNKS])
    load.start()
    pl.semaphore_wait(barrier, 4 + PEERS - 1)

    def send(j, n, view, device):
        pltpu.make_async_remote_copy(
            src_ref=view, dst_ref=view, send_sem=g_send.at[j, n], recv_sem=g_recv.at[j, n],
            device_id=device, device_id_type=MESH,
        ).start()

    def landed(j, n, view):
        pltpu.make_async_remote_copy(
            src_ref=view, dst_ref=view, send_sem=g_send.at[j, n], recv_sem=g_recv.at[j, n],
            device_id=sibling, device_id_type=MESH,
        ).wait_recv()

    low, high = pl.ds(0, 64), pl.ds(64, 64)
    first, second = pl.ds(0, 2), pl.ds(2, 2)

    def own_blocks(j):
        own[j].wait()
        send(j, 0, gathered.at[j, y, x, core, 0], to_x_up)
        send(j, 1, gathered.at[j, y, x, core, 0], to_x_down)
        send(j, 2, gathered.at[j, y, x, core, 1], to_y_up)
        send(j, 3, gathered.at[j, y, x, core, 1], to_y_down)

    def pass_blocks(j):
        landed(j, 0, gathered.at[j, y, x_down, core, 0])
        send(j, 4, gathered.at[j, y, x_down, core, 0, low], to_x_up)
        landed(j, 1, gathered.at[j, y, x_up, core, 0])
        send(j, 5, gathered.at[j, y, x_up, core, 0, high], to_x_down)
        landed(j, 2, gathered.at[j, y_down, x, core, 1])
        send(j, 6, gathered.at[j, y_down, x, core, 1, low], to_y_up)
        landed(j, 3, gathered.at[j, y_up, x, core, 1])
        send(j, 7, gathered.at[j, y_up, x, core, 1, high], to_y_down)

    def own_lines(j):
        landed(j, 4, gathered.at[j, y, x_far, core, 0, low])
        landed(j, 5, gathered.at[j, y, x_far, core, 0, high])
        send(j, 8, gathered.at[j, y, :, core, 0], to_y_up)
        send(j, 9, gathered.at[j, y, :, core, 0], to_y_down)
        landed(j, 6, gathered.at[j, y_far, x, core, 1, low])
        landed(j, 7, gathered.at[j, y_far, x, core, 1, high])
        send(j, 10, gathered.at[j, :, x, core, 1], to_x_up)
        send(j, 11, gathered.at[j, :, x, core, 1], to_x_down)
        send(j, 16, gathered.at[j, y, :, core, 0], sibling)
        send(j, 20, gathered.at[j, :, x, core, 1], sibling)

    def pass_lines(j):
        landed(j, 8, gathered.at[j, y_down, :, core, 0])
        send(j, 12, gathered.at[j, y_down, first, core, 0], to_y_up)
        landed(j, 9, gathered.at[j, y_up, :, core, 0])
        send(j, 13, gathered.at[j, y_up, second, core, 0], to_y_down)
        landed(j, 10, gathered.at[j, :, x_down, core, 1])
        send(j, 14, gathered.at[j, first, x_down, core, 1], to_x_up)
        landed(j, 11, gathered.at[j, :, x_up, core, 1])
        send(j, 15, gathered.at[j, second, x_up, core, 1], to_x_down)
        send(j, 17, gathered.at[j, y_down, :, core, 0], sibling)
        send(j, 18, gathered.at[j, y_up, :, core, 0], sibling)
        send(j, 21, gathered.at[j, :, x_down, core, 1], sibling)
        send(j, 22, gathered.at[j, :, x_up, core, 1], sibling)

    def last_lines(j):
        landed(j, 12, gathered.at[j, y_far, first, core, 0])
        landed(j, 13, gathered.at[j, y_far, second, core, 0])
        send(j, 19, gathered.at[j, y_far, :, core, 0], sibling)
        landed(j, 14, gathered.at[j, first, x_far, core, 1])
        landed(j, 15, gathered.at[j, second, x_far, core, 1])
        send(j, 23, gathered.at[j, :, x_far, core, 1], sibling)

    def from_sibling(j):
        other = 1 - core
        for n, line in ((16, y), (17, y_down), (18, y_up), (19, y_far)):
            landed(j, n, gathered.at[j, line, :, other, 0])
        for n, line in ((20, x), (21, x_down), (22, x_up), (23, x_far)):
            landed(j, n, gathered.at[j, :, line, other, 1])

    def all_sent(j):
        for n, rows in ((0, 1), (1, 1), (2, 1), (3, 1)):
            view = gathered.at[j, y, x, core, 0]
            pltpu.make_async_copy(view, view, g_send.at[j, n]).wait()
        for n in (4, 5, 6, 7):
            view = gathered.at[j, y, x, core, 0, low]
            pltpu.make_async_copy(view, view, g_send.at[j, n]).wait()
        for n in (8, 9, 10, 11, 16, 17, 18, 19, 20, 21, 22, 23):
            view = gathered.at[j, y, :, core, 0]
            pltpu.make_async_copy(view, view, g_send.at[j, n]).wait()
        for n in (12, 13, 14, 15):
            view = gathered.at[j, y, first, core, 0]
            pltpu.make_async_copy(view, view, g_send.at[j, n]).wait()

    def plan():
        goal = target[...]
        shard, slot = goal >> 12, goal & (ROWS - 1)
        chosen = lax.broadcasted_iota(jnp.int32, (PEERS, ROWS), 0) == shard
        onehot = chosen.astype(jnp.float32)
        earlier = (
            lax.broadcasted_iota(jnp.int32, (ROWS, ROWS), 0)
            < lax.broadcasted_iota(jnp.int32, (ROWS, ROWS), 1)
        ).astype(jnp.bfloat16)
        before = nn(onehot.astype(jnp.bfloat16), earlier)
        rank = jnp.sum(onehot * before, axis=0, keepdims=True).astype(jnp.int32)
        bucket = shard * CAPACITY + rank
        spread[...] = (
            lax.broadcasted_iota(jnp.int32, (PEERS * CAPACITY, ROWS), 0) == bucket
        ).astype(jnp.bfloat16)
        lane = rank + CAPACITY * lax.rem(dp, 4)
        place = (lax.broadcasted_iota(jnp.int32, (128, ROWS), 0) == lane).astype(jnp.bfloat16)
        marks = (onehot * (slot + 1).astype(jnp.float32)).astype(jnp.bfloat16)
        table = nt(marks, place)
        slots_out[...] = jnp.broadcast_to(table[:, None, :], (PEERS, 8, 128))

        def ship(k, carry):
            peer = lax.rem(dp + k, PEERS)
            pltpu.make_async_remote_copy(
                src_ref=slots_out.at[peer], dst_ref=slots_in.at[dp],
                send_sem=s_send.at[k], recv_sem=s_recv.at[k],
                device_id=(peer, fsdp), device_id_type=MESH,
            ).start()
            return carry

        lax.fori_loop(1, PEERS, ship, 0)
        slots_in[dp] = slots_out[dp]

        ids = jnp.broadcast_to(segment[...].astype(jnp.float32), (ROWS, ROWS))
        causal = lax.broadcasted_iota(jnp.int32, (ROWS, ROWS), 1) <= lax.broadcasted_iota(
            jnp.int32, (ROWS, ROWS), 0
        )
        mask[...] = ((ids == ids.T) & causal).astype(jnp.float32)

    def plan_arrivals():
        def wait(k, carry):
            source = lax.rem(dp + PEERS - k, PEERS)
            copy = pltpu.make_async_remote_copy(
                src_ref=slots_out.at[source], dst_ref=slots_in.at[source],
                send_sem=s_send.at[k], recv_sem=s_recv.at[k],
                device_id=(source, fsdp), device_id_type=MESH,
            )
            copy.wait_recv()
            copy.wait_send()
            return carry

        lax.fori_loop(1, PEERS, wait, 0)
        wanted = lax.broadcasted_iota(jnp.int32, (ROWS, 128), 0) + 1
        for t in range(4):
            row = slots_in[4 * t] + slots_in[4 * t + 1] + slots_in[4 * t + 2] + slots_in[4 * t + 3]
            row = row[0:1].astype(jnp.int32)
            collect[:, t * 128 : (t + 1) * 128] = (wanted == row).astype(jnp.bfloat16)

    def normalise():
        load.wait()

        def some(i, carry):
            rows = pl.ds(pl.multiple_of(i * 16, 16), 16)
            floats = normed[rows, :].astype(jnp.float32)
            scale = lax.rsqrt(jnp.mean(floats * floats, axis=1, keepdims=True) + EPS)
            normed[rows, :] = (floats * scale * gain[...]).astype(jnp.bfloat16)
            return carry

        lax.fori_loop(0, ROWS // 16, some, 0)

    def project(j):
        total[...] = jnp.zeros_like(total)

        def some(i, carry):
            columns = pl.ds(pl.multiple_of(i * 2048, 2048), 2048)
            block = gathered[j, i].reshape(2048, WIDTH)
            total[...] += nn(normed[:, columns], block)
            return carry

        lax.fori_loop(0, 4, some, 0)

    def attend(j):
        n = j - 1
        contexts = []
        for h in range(2):
            query = total[:, h * HEAD : (h + 1) * HEAD].astype(jnp.bfloat16)
            scores = nt(query, keys[...]) * HEAD ** (-0.5)
            scores = jnp.where(mask[...] > 0.5, scores, -1e30)
            expos = jnp.exp(scores - jnp.max(scores, axis=1, keepdims=True))
            weights = (expos / jnp.sum(expos, axis=1, keepdims=True)).astype(jnp.bfloat16)
            contexts.append(nn(weights, values[...]).astype(jnp.bfloat16))
        context = jnp.concatenate(contexts, axis=1)
        outgoing[n] = nn(spread[...], context).astype(jnp.bfloat16).reshape(PEERS, CAPACITY, WIDTH)

        def ship(k, carry):
            peer = lax.rem(dp + k, PEERS)
            pltpu.make_async_remote_copy(
                src_ref=outgoing.at[n, peer], dst_ref=incoming.at[n, dp],
                send_sem=a_send.at[n, k], recv_sem=a_recv.at[n, k],
                device_id=(peer, fsdp), device_id_type=MESH,
            ).start()
            return carry

        lax.fori_loop(1, PEERS, ship, 0)
        incoming[n, dp] = outgoing[n, dp]

    def deliver(j):
        n = j - 1

        def wait(k, carry):
            source = lax.rem(dp + PEERS - k, PEERS)
            copy = pltpu.make_async_remote_copy(
                src_ref=outgoing.at[n, source], dst_ref=incoming.at[n, source],
                send_sem=a_send.at[n, k], recv_sem=a_recv.at[n, k],
                device_id=(source, fsdp), device_id_type=MESH,
            )
            copy.wait_recv()
            copy.wait_send()
            return carry

        lax.fori_loop(1, PEERS, wait, 0)
        rows = incoming[n].reshape(PEERS * CAPACITY, WIDTH)
        out[:, n * WIDTH : (n + 1) * WIDTH] = nn(collect[...], rows).astype(jnp.bfloat16)

    def compute(j):
        from_sibling(j)
        project(j)
        if j == 0:
            keys[...] = total[:, :HEAD].astype(jnp.bfloat16)
            values[...] = total[:, HEAD:].astype(jnp.bfloat16)
        else:
            attend(j)

    own_blocks(0)
    own_blocks(1)
    plan()
    pass_blocks(0)
    own_lines(0)
    for j in range(CHUNKS):
        if j + 1 < CHUNKS:
            pass_blocks(j + 1)
        if j == 0:
            normalise()
        if j + 1 < CHUNKS:
            own_lines(j + 1)
        if j + 2 < CHUNKS:
            own_blocks(j + 2)
        pass_lines(j)
        if j == 0:
            plan_arrivals()
        if j >= 1:
            compute(j - 1)
        last_lines(j)
    compute(CHUNKS - 1)
    for j in range(1, CHUNKS):
        deliver(j)
    for j in range(CHUNKS):
        all_sent(j)


def per_device(hidden, gain, qkv_weight, owner_segment, target_row):
    any_space = pl.BlockSpec(memory_space=pl.ANY)
    vmem = pl.BlockSpec(memory_space=pltpu.VMEM)
    bf16, f32 = jnp.bfloat16, jnp.float32
    dma = pltpu.SemaphoreType.DMA
    return pl.pallas_call(
        kernel,
        out_shape=jax.ShapeDtypeStruct((ROWS, QUERIES * WIDTH), bf16),
        in_specs=[any_space, vmem, any_space, vmem, vmem],
        out_specs=vmem,
        scratch_shapes=[
            pltpu.VMEM((CHUNKS, 4, 4, 2, 2, 128, WIDTH), bf16),
            pltpu.VMEM((ROWS, FEATURES), bf16),
            pltpu.VMEM((ROWS, WIDTH), f32),
            pltpu.VMEM((ROWS, HEAD), bf16),
            pltpu.VMEM((ROWS, HEAD), bf16),
            pltpu.VMEM((ROWS, ROWS), f32),
            pltpu.VMEM((PEERS * CAPACITY, ROWS), bf16),
            pltpu.VMEM((ROWS, PEERS * CAPACITY), bf16),
            pltpu.VMEM((QUERIES, PEERS, CAPACITY, WIDTH), bf16),
            pltpu.VMEM((QUERIES, PEERS, CAPACITY, WIDTH), bf16),
            pltpu.VMEM((PEERS, 8, 128), f32),
            pltpu.VMEM((PEERS, 8, 128), f32),
            dma((CHUNKS + 1,)),
            dma((CHUNKS, 24)),
            dma((CHUNKS, 24)),
            dma((QUERIES, PEERS)),
            dma((QUERIES, PEERS)),
            dma((PEERS,)),
            dma((PEERS,)),
        ],
        compiler_params=pltpu.CompilerParams(
            collective_id=0, has_side_effects=True, vmem_limit_bytes=56 << 20
        ),
        cost_estimate=pl.CostEstimate(
            flops=2 * ROWS * FEATURES * 1280, bytes_accessed=6 << 20, transcendentals=8 * ROWS * ROWS
        ),
    )(
        hidden,
        gain.reshape(1, FEATURES),
        qkv_weight.reshape(2, 2, 128, 1280),
        owner_segment.reshape(1, ROWS),
        target_row.reshape(1, ROWS),
    )


def solution(mesh):
    in_specs = (P(("dp", "fsdp"), None), P(), P("fsdp", None), P(("dp", "fsdp")), P(("dp", "fsdp")))
    out_specs = P(("dp", "fsdp"), None)
    return jax.shard_map(
        per_device, mesh=mesh, in_specs=in_specs, out_specs=out_specs, check_vma=False
    )
```

time: 222 us -> 100 us (0.45)
  waiting for transfers between devices: 139 us -> 0 us
  Pallas kernels: 0 us -> 98.2 us
  starting transfers between devices: 27 us -> 0 us
  local copies, waits for them, and re-layouts: 19.2 us -> 1.87 us
  matrix products: 15.5 us -> 0 us
  between operations: 13.5 us -> 0.01 us
  other arithmetic: 7.38 us -> 0 us
    all_gather x1 -> x0, waiting for transfers between devices: 106 us -> none  [per_device(): lax.all_gather(qkv_weight, 'fsdp', axis=0, tiled=True)]
    pallas_call x0 -> x1, Pallas kernels: none -> 98.2 us  [per_device(): pl.pallas_call(kernel, out_shape=jax.ShapeDtypeStruct((ROWS, QUERIES * WI...]
    all_to_all x4 -> x0, waiting for transfers between devices: 31.9 us -> none  [the longest x1 25.2 us: per_device(): lax.all_to_all(buffer.reshape(dp_size, capacity, projected.shape[1]), 'dp...]
    all_to_all x4 -> x0, starting transfers between devices: 27 us -> none  [the longest x1 9.98 us: per_device(): lax.all_to_all(pack_ints(seg_key, 0), 'dp', split_axis=0, concat_axis=0,...]
    scatter x7 -> x0, local copies, waits for them, and re-layouts: 15 us -> none  [the longest x3 7.91 us: place(): return jnp.zeros((count,) + flat.shape[1:], flat.dtype).at[arrived.reshap...]
    dot_general x2 -> x0, matrix products: 14.7 us -> none  [the longest x1 13.6 us: per_device(): jnp.dot(normed, lax.all_gather(qkv_weight, 'fsdp', axis=0, tiled=True), p...]
    reduce_sum x2 -> x0, other arithmetic: 3.2 us -> none  [the longest x1 3.11 us: per_device(): jnp.mean(floats * floats, axis=1, keepdims=True) + EPS]
    all_to_all x4 -> x0, local copies, waits for them, and re-layouts: 2.54 us -> none  [the longest x2 1.19 us: per_device(): lax.all_to_all(slots, 'dp', split_axis=0, concat_axis=0, tiled=True)]
  transfers between devices with their start and end apart: 5 -> 0, of which waited for: 4 -> 0; matrix products, arithmetic and copies ran while one was open for 15% -> 0% of each run, Pallas kernels for 0% -> 0%
where the time goes in v1:
time: 100 us
  Pallas kernels  98.2 us (98%)
  local copies, waits for them, and re-layouts  1.87 us (2%)
    pallas_call x1, Pallas kernels, per_device(): pl.pallas_call(kernel, out_shape=jax.ShapeDtypeStruct((ROWS, QUERIES * WI...  98.2 us

profile of v1, /device:TPU:1, one launch (start us, length us, event | category | flops | bytes accessed | tf_op | source)
XLA Modules:
  0.0 100.1 jit_solution(3353670098307387485)
XLA Ops:
  0.0 98.2 %shard_map.55 = bf16[256,1024]{1,0:T(8,128)(2,1)} custom-call(bf16[256,8192]{1,0:T(8,128)(2,1)} %hidden.1, f32[1,8192]{1,0:T(1,128)} %bitcast.5, bf16[2,2,128,1280]{3,2,1,0:T(8,128)(2,1)} %bitcast.4, s32[1,256]{1,0:T(1,128)} %bitcast.6, s32[1,256]{1,0:T(1,128)} %bitcast.7), custom_call_target="tpu_custom_call" | custom-call | flops 5368709120 | bytes 6291456 | tf_op jit(solution)/shard_map/pallas_call | solution.py:321
  98.3 1.9 %copy.7 = bf16[256,1024]{1,0:T(8,128)(2,1)} copy(bf16[256,1024]{1,0:T(8,128)(2,1)} %shard_map.55) | data formatting | bytes 1048576

commit v2 on v0

v2 whole, which is shorter than its diff:
```python
import jax
import jax.numpy as jnp
from jax import lax
from jax.experimental import pallas as pl
from jax.experimental.pallas import tpu as pltpu
from jax.sharding import PartitionSpec as P

MESH = pl.DeviceIdType.MESH
HEAD = 128
EPS = 1e-05
ROWS = 256
FEATURES = 8192
PEERS = 16
CAPACITY = 32
CHUNKS = ((1024, 256), (0, 256), (512, 256), (768, 128), (896, 128))
RING = (256, 256)
COLUMNS = 1024
NEAR, FAR, LINE, LAST, TWIN, TWIN_LAST = range(6)


def nt(a, b):
    return lax.dot_general(a, b, (((1,), (1,)), ((), ())), preferred_element_type=jnp.float32)


def nn(a, b):
    return jnp.dot(a, b, preferred_element_type=jnp.float32)


def kernel(
    hidden, gain, weight, segment, target, out,
    wide, narrow, ring, raw, normed, total, keys, values, mask, spread, collect,
    out_wide, in_wide, out_narrow, in_narrow, slots_out, slots_in,
    local_sem, g_send, g_recv, z_send, z_recv, a_send, a_recv, s_sem,
):
    dp, fsdp = lax.axis_index("dp"), lax.axis_index("fsdp")
    z, core = dp // 2, lax.rem(dp, 2)
    y, x = fsdp // 4, lax.rem(fsdp, 4)
    other = 1 - core
    x_up, x_down, x_far = lax.rem(x + 1, 4), lax.rem(x + 3, 4), lax.rem(x + 2, 4)
    y_up, y_down, y_far = lax.rem(y + 1, 4), lax.rem(y + 3, 4), lax.rem(y + 2, 4)
    to_x_up, to_x_down = (dp, y * 4 + x_up), (dp, y * 4 + x_down)
    to_y_up, to_y_down = (dp, y_up * 4 + x), (dp, y_down * 4 + x)
    to_z_up = (lax.rem(z + 1, 8) * 2 + core, fsdp)
    to_z_down = (lax.rem(z + 7, 8) * 2 + core, fsdp)
    sibling = (dp + other - core, fsdp)

    def chunk(j):
        return wide.at[j] if j < 3 else narrow.at[j - 3]

    barrier = pltpu.get_barrier_semaphore()

    def greet(k, carry):
        for peer in ((lax.rem(dp + k, PEERS), fsdp), (dp, lax.rem(fsdp + k, PEERS))):
            pl.semaphore_signal(barrier, inc=1, device_id=peer, device_id_type=MESH)
        return carry

    lax.fori_loop(1, PEERS, greet, 0)

    load = pltpu.make_async_copy(hidden, raw, local_sem.at[0])
    load.start()
    ring_half, ring_part = z // 4, lax.rem(z, 4)
    ring_place = (1 - ring_half) * (y * 4 + x) + ring_half * (x * 4 + y)
    own_ring = pltpu.make_async_copy(
        weight.at[core, ring_half, ring_part, :, pl.ds(*RING)],
        ring.at[ring_half, core, ring_place, ring_part],
        local_sem.at[1],
    )
    own_ring.start()
    own = []
    for j, (start, width) in enumerate(CHUNKS):
        for half, (line, place) in enumerate(((y, x), (x, y))):
            copy = pltpu.make_async_copy(
                weight.at[core, half, :, :, pl.ds(start, width)],
                chunk(j).at[half, core, line, place],
                local_sem.at[2 + 2 * j + half],
            )
            copy.start()
            own.append(copy)

    def send(view, device, send_sem, recv_sem):
        pltpu.make_async_remote_copy(
            src_ref=view, dst_ref=view, send_sem=send_sem, recv_sem=recv_sem,
            device_id=device, device_id_type=MESH,
        ).start()

    def landed(view, sem):
        pltpu.make_async_copy(view, view, sem).wait()

    low, high = pl.ds(0, 2), pl.ds(2, 2)

    def near(j):
        g, s, r = chunk(j), g_send.at[j], g_recv.at[j, NEAR]
        own[2 * j].wait()
        own[2 * j + 1].wait()
        send(g.at[0, core, y, x], to_x_up, s, r)
        send(g.at[0, core, y, x], to_x_down, s, r)
        send(g.at[1, core, x, y], to_y_up, s, r)
        send(g.at[1, core, x, y], to_y_down, s, r)

    def far(j):
        g, s, r = chunk(j), g_send.at[j], g_recv.at[j, FAR]
        landed(g.at[0, core, y], g_recv.at[j, NEAR])
        send(g.at[0, core, y, x_down, low], to_x_up, s, r)
        send(g.at[0, core, y, x_up, high], to_x_down, s, r)
        send(g.at[1, core, x, y_down, low], to_y_up, s, r)
        send(g.at[1, core, x, y_up, high], to_y_down, s, r)

    def lines(j):
        g, s, r, t = chunk(j), g_send.at[j], g_recv.at[j, LINE], g_recv.at[j, TWIN]
        landed(g.at[0, core, y, low], g_recv.at[j, FAR])
        send(g.at[0, core, y], to_y_up, s, r)
        send(g.at[0, core, y], to_y_down, s, r)
        send(g.at[1, core, x], to_x_up, s, r)
        send(g.at[1, core, x], to_x_down, s, r)
        send(g.at[0, core, y], sibling, s, t)
        send(g.at[1, core, x], sibling, s, t)

    def pass_lines(j):
        g, s, r, t = chunk(j), g_send.at[j], g_recv.at[j, LAST], g_recv.at[j, TWIN]
        landed(g.at[0, core], g_recv.at[j, LINE])
        send(g.at[0, core, y_down, low], to_y_up, s, r)
        send(g.at[0, core, y_up, high], to_y_down, s, r)
        send(g.at[1, core, x_down, low], to_x_up, s, r)
        send(g.at[1, core, x_up, high], to_x_down, s, r)
        send(g.at[0, core, y_down], sibling, s, t)
        send(g.at[0, core, y_up], sibling, s, t)
        send(g.at[1, core, x_down], sibling, s, t)
        send(g.at[1, core, x_up], sibling, s, t)

    def last_lines(j):
        g, s, t = chunk(j), g_send.at[j], g_recv.at[j, TWIN_LAST]
        landed(g.at[0, core, low], g_recv.at[j, LAST])
        send(g.at[0, core, y_far], sibling, s, t)
        send(g.at[1, core, x_far], sibling, s, t)

    def twin(j):
        landed(chunk(j).at[:, other, pl.ds(0, 3)], g_recv.at[j, TWIN])

    def twin_last(j):
        landed(chunk(j).at[:, other, 0], g_recv.at[j, TWIN_LAST])

    def ring_at(where, places=None):
        place = slice(None) if places is None else places
        return ring.at[where // 4, core, place, lax.rem(where, 4)]

    halves = (pl.ds(0, 8), pl.ds(8, 8))

    def z_up(n):
        return lax.rem(z + n, 8)

    def z_down(n):
        return lax.rem(z + 8 - n, 8)

    def plane():
        own_ring.wait()
        view = ring.at[ring_half, core, ring_place, ring_part]

        def ship(k, carry):
            send(view, (dp, lax.rem(fsdp + k, PEERS)), z_send.at[0], z_recv.at[0])
            return carry

        lax.fori_loop(1, PEERS, ship, 0)

    def ring_start():
        landed(ring_at(z, pl.ds(0, 15)), z_recv.at[0])
        for h in range(2):
            send(ring_at(z, halves[h]), to_z_up, z_send.at[1], z_recv.at[2 + h])
            send(ring_at(z, halves[h]), to_z_down, z_send.at[1], z_recv.at[2 + h])
        send(ring_at(z), sibling, z_send.at[1], z_recv.at[1])

    def ring_step(n, h):
        landed(ring_at(z), z_recv.at[2 * n + h])
        sem = z_recv.at[2 * n + 2 + h]
        if n < 3 or h == 0:
            send(ring_at(z_down(n), halves[h]), to_z_up, z_send.at[1], sem if n < 3 else z_recv.at[8])
        if n < 3 or h == 1:
            send(ring_at(z_up(n), halves[h]), to_z_down, z_send.at[1], sem if n < 3 else z_recv.at[8])
        if h == 1:
            send(ring_at(z_down(n)), sibling, z_send.at[1], z_recv.at[1])
            send(ring_at(z_up(n)), sibling, z_send.at[1], z_recv.at[1])

    def ring_end():
        landed(ring_at(z), z_recv.at[8])
        send(ring_at(z_up(4)), sibling, z_send.at[1], z_recv.at[1])

    def ring_twin():
        landed(ring.at[:, other], z_recv.at[1])

    def plan():
        goal = target[...]
        shard, slot = goal >> 12, goal & (ROWS - 1)
        chosen = lax.broadcasted_iota(jnp.int32, (PEERS, ROWS), 0) == shard
        onehot = chosen.astype(jnp.float32)
        earlier = (
            lax.broadcasted_iota(jnp.int32, (ROWS, ROWS), 0)
            < lax.broadcasted_iota(jnp.int32, (ROWS, ROWS), 1)
        ).astype(jnp.bfloat16)
        before = nn(onehot.astype(jnp.bfloat16), earlier)
        rank = jnp.sum(onehot * before, axis=0, keepdims=True).astype(jnp.int32)
        bucket = shard * CAPACITY + rank
        spread[...] = (
            lax.broadcasted_iota(jnp.int32, (PEERS * CAPACITY, ROWS), 0) == bucket
        ).astype(jnp.bfloat16)
        lane = rank + CAPACITY * lax.rem(dp, 4)
        place = (lax.broadcasted_iota(jnp.int32, (128, ROWS), 0) == lane).astype(jnp.bfloat16)
        marks = (onehot * (slot + 1).astype(jnp.float32)).astype(jnp.bfloat16)
        table = nt(marks, place)
        slots_out[...] = jnp.broadcast_to(table[:, None, :], (PEERS, 8, 128))
        ids = jnp.broadcast_to(segment[...].astype(jnp.float32), (ROWS, ROWS))
        causal = lax.broadcasted_iota(jnp.int32, (ROWS, ROWS), 1) <= lax.broadcasted_iota(
            jnp.int32, (ROWS, ROWS), 0
        )
        mask[...] = ((ids == ids.T) & causal).astype(jnp.float32)

    def to_peers(source, landing, send_sem, recv_sem):
        def ship(k, carry):
            peer = lax.rem(dp + k, PEERS)
            pltpu.make_async_remote_copy(
                src_ref=source.at[peer], dst_ref=landing.at[dp],
                send_sem=send_sem, recv_sem=recv_sem,
                device_id=(peer, fsdp), device_id_type=MESH,
            ).start()
            return carry

        lax.fori_loop(1, PEERS, ship, 0)
        landing[dp] = source[dp]

    def from_peers(landing, recv_sem):
        landed(landing.at[pl.ds(0, PEERS - 1)], recv_sem)

    def plan_arrivals():
        from_peers(slots_in, s_sem.at[1])
        wanted = lax.broadcasted_iota(jnp.int32, (ROWS, 128), 0) + 1
        for t in range(4):
            row = slots_in[4 * t] + slots_in[4 * t + 1] + slots_in[4 * t + 2] + slots_in[4 * t + 3]
            row = row[0:1].astype(jnp.int32)
            collect[:, t * 128 : (t + 1) * 128] = (wanted == row).astype(jnp.bfloat16)

    def normalise():
        def some(i, carry):
            rows = pl.ds(pl.multiple_of(i * 16, 16), 16)
            floats = raw[rows, :].astype(jnp.float32)
            scale = lax.rsqrt(jnp.mean(floats * floats, axis=1, keepdims=True) + EPS)
            for shard in range(16):
                for c in range(2):
                    for half in range(2):
                        a = shard * 512 + c * 256 + half * 128
                        at = (1 - half) * shard + half * (shard % 4 * 4 + shard // 4)
                        b = ((half * 2 + c) * 16 + at) * 128
                        part = raw[rows, a : a + 128].astype(jnp.float32)
                        normed[rows, b : b + 128] = (part * scale * gain[:, a : a + 128]).astype(
                            jnp.bfloat16
                        )
            return carry

        lax.fori_loop(0, ROWS // 16, some, 0)

    def project(g, width):
        total[:, :width] = jnp.zeros((ROWS, width), jnp.float32)

        def some(i, carry):
            columns = pl.ds(pl.multiple_of(i * 2048, 2048), 2048)
            block = g[i // 2, lax.rem(i, 2)].reshape(2048, width)
            total[:, :width] += nn(normed[:, columns], block)
            return carry

        lax.fori_loop(0, 4, some, 0)

    def project_lines(j, mine, width):
        g = chunk(j)
        sums = jnp.zeros((ROWS, width), jnp.float32)
        for half in range(2):
            for c in range(2):
                for line in mine[half]:
                    first = ((half * 2 + c) * 16 + line * 4) * 128
                    columns = pl.ds(pl.multiple_of(first, 512), 512)
                    sums = sums + nn(normed[:, columns], g[half, c, line].reshape(512, width))
        return sums

    def project_first(j, width):
        total[:, :width] = project_lines(j, ((y, y_up, y_down), (x, x_up, x_down)), width)

    def project_last(j, width):
        total[:, :width] += project_lines(j, ((y_far,), (x_far,)), width)

    def group(n):
        if n < 3:
            return out_wide.at[n], in_wide.at[n], 256, (RING[0], 0, 512)[n]
        return out_narrow.at[n - 3], in_narrow.at[n - 3], 128, (768, 896)[n - 3]

    def attend(n):
        outgoing, incoming, width, start = group(n)
        contexts = []
        for h in range(width // HEAD):
            query = total[:, h * HEAD : (h + 1) * HEAD].astype(jnp.bfloat16)
            scores = nt(query, keys[...]) * HEAD ** (-0.5)
            scores = jnp.where(mask[...] > 0.5, scores, -1e30)
            expos = jnp.exp(scores - jnp.max(scores, axis=1, keepdims=True))
            weights = (expos / jnp.sum(expos, axis=1, keepdims=True)).astype(jnp.bfloat16)
            contexts.append(nn(weights, values[...]).astype(jnp.bfloat16))
        context = jnp.concatenate(contexts, axis=1) if len(contexts) > 1 else contexts[0]
        outgoing[...] = nn(spread[...], context).astype(jnp.bfloat16).reshape(PEERS, CAPACITY, width)
        to_peers(outgoing, incoming, a_send.at[n], a_recv.at[n])

    def deliver(n):
        outgoing, incoming, width, start = group(n)
        from_peers(incoming, a_recv.at[n])
        rows = incoming[...].reshape(PEERS * CAPACITY, width)
        out[:, start : start + width] = nn(collect[...], rows).astype(jnp.bfloat16)

    plan()
    load.wait()
    normalise()
    pl.semaphore_wait(barrier, 2 * (PEERS - 1))

    plane()
    near(0)
    near(1)
    near(2)
    to_peers(slots_out, slots_in, s_sem.at[0], s_sem.at[1])
    ring_start()
    far(0)
    near(3)
    near(4)
    far(1)
    far(2)
    lines(0)
    far(3)
    far(4)
    ring_step(1, 0)
    lines(1)
    ring_step(1, 1)
    plan_arrivals()
    ring_step(2, 0)
    pass_lines(0)
    lines(2)
    ring_step(2, 1)
    ring_step(3, 0)
    pass_lines(1)
    ring_step(3, 1)
    last_lines(0)
    lines(3)
    twin(0)
    twin_last(0)
    project(chunk(0), 256)
    keys[...] = total[:, :HEAD].astype(jnp.bfloat16)
    values[...] = total[:, HEAD:].astype(jnp.bfloat16)
    ring_end()
    ring_twin()
    project(ring, 256)
    pass_lines(2)
    lines(4)
    attend(0)
    last_lines(1)
    twin(1)
    twin_last(1)
    project(chunk(1), 256)
    pass_lines(3)
    attend(1)
    last_lines(2)
    twin(2)
    twin_last(2)
    project(chunk(2), 256)
    pass_lines(4)
    attend(2)
    twin(3)
    project_first(3, 128)
    last_lines(3)
    twin_last(3)
    project_last(3, 128)
    attend(3)
    twin(4)
    project_first(4, 128)
    last_lines(4)
    twin_last(4)
    project_last(4, 128)
    attend(4)
    for n in range(5):
        deliver(n)
    for j, (start, width) in enumerate(CHUNKS):
        landed(raw.at[pl.ds(0, width), pl.ds(0, 7936)], g_send.at[j])
    landed(raw.at[pl.ds(0, 16), pl.ds(0, 7680)], z_send.at[0])
    landed(raw.at[pl.ds(0, 240)], z_send.at[1])
    landed(slots_out.at[pl.ds(0, PEERS - 1)], s_sem.at[0])
    for n in range(5):
        landed(group(n)[0].at[pl.ds(0, PEERS - 1)], a_send.at[n])


def per_device(hidden, gain, qkv_weight, owner_segment, target_row):
    any_space = pl.BlockSpec(memory_space=pl.ANY)
    vmem = pl.BlockSpec(memory_space=pltpu.VMEM)
    bf16, f32 = jnp.bfloat16, jnp.float32
    dma = pltpu.SemaphoreType.DMA
    return pl.pallas_call(
        kernel,
        out_shape=jax.ShapeDtypeStruct((ROWS, COLUMNS), bf16),
        in_specs=[any_space, vmem, any_space, vmem, vmem],
        out_specs=vmem,
        scratch_shapes=[
            pltpu.VMEM((3, 2, 2, 4, 4, 4, 32, 256), bf16),
            pltpu.VMEM((2, 2, 2, 4, 4, 4, 32, 128), bf16),
            pltpu.VMEM((2, 2, 16, 4, 32, 256), bf16),
            pltpu.VMEM((ROWS, FEATURES), bf16),
            pltpu.VMEM((ROWS, FEATURES), bf16),
            pltpu.VMEM((ROWS, 256), f32),
            pltpu.VMEM((ROWS, HEAD), bf16),
            pltpu.VMEM((ROWS, HEAD), bf16),
            pltpu.VMEM((ROWS, ROWS), f32),
            pltpu.VMEM((PEERS * CAPACITY, ROWS), bf16),
            pltpu.VMEM((ROWS, PEERS * CAPACITY), bf16),
            pltpu.VMEM((3, PEERS, CAPACITY, 256), bf16),
            pltpu.VMEM((3, PEERS, CAPACITY, 256), bf16),
            pltpu.VMEM((2, PEERS, CAPACITY, 128), bf16),
            pltpu.VMEM((2, PEERS, CAPACITY, 128), bf16),
            pltpu.VMEM((PEERS, 8, 128), f32),
            pltpu.VMEM((PEERS, 8, 128), f32),
            dma((2 + 2 * len(CHUNKS),)),
            dma((len(CHUNKS),)),
            dma((len(CHUNKS), 6)),
            dma((2,)),
            dma((9,)),
            dma((5,)),
            dma((5,)),
            dma((2,)),
        ],
        compiler_params=pltpu.CompilerParams(
            collective_id=0, has_side_effects=True, vmem_limit_bytes=56 << 20
        ),
        cost_estimate=pl.CostEstimate(
            flops=2 * ROWS * FEATURES * 1280, bytes_accessed=6 << 20, transcendentals=8 * ROWS * ROWS
        ),
    )(
        hidden,
        gain.reshape(1, FEATURES),
        qkv_weight.reshape(2, 2, 4, 32, 1280),
        owner_segment.reshape(1, ROWS),
        target_row.reshape(1, ROWS),
    )


def solution(mesh):
    in_specs = (P(("dp", "fsdp"), None), P(), P("fsdp", None), P(("dp", "fsdp")), P(("dp", "fsdp")))
    out_specs = P(("dp", "fsdp"), None)
    return jax.shard_map(
        per_device, mesh=mesh, in_specs=in_specs, out_specs=out_specs, check_vma=False
    )
```

time: 222 us -> 80.4 us (0.36)
  waiting for transfers between devices: 139 us -> 0 us
  Pallas kernels: 0 us -> 78.3 us
  starting transfers between devices: 27 us -> 0 us
  local copies, waits for them, and re-layouts: 19.2 us -> 1.87 us
  matrix products: 15.5 us -> 0 us
  between operations: 13.5 us -> 0.01 us
  other arithmetic: 7.38 us -> 0 us
    all_gather x1 -> x0, waiting for transfers between devices: 106 us -> none  [per_device(): lax.all_gather(qkv_weight, 'fsdp', axis=0, tiled=True)]
    pallas_call x0 -> x1, Pallas kernels: none -> 78.3 us  [per_device(): pl.pallas_call(kernel, out_shape=jax.ShapeDtypeStruct((ROWS, COLUMNS), bf...]
    all_to_all x4 -> x0, waiting for transfers between devices: 31.9 us -> none  [the longest x1 25.2 us: per_device(): lax.all_to_all(buffer.reshape(dp_size, capacity, projected.shape[1]), 'dp...]
    all_to_all x4 -> x0, starting transfers between devices: 27 us -> none  [the longest x1 9.98 us: per_device(): lax.all_to_all(pack_ints(seg_key, 0), 'dp', split_axis=0, concat_axis=0,...]
    scatter x7 -> x0, local copies, waits for them, and re-layouts: 15 us -> none  [the longest x3 7.91 us: place(): return jnp.zeros((count,) + flat.shape[1:], flat.dtype).at[arrived.reshap...]
    dot_general x2 -> x0, matrix products: 14.7 us -> none  [the longest x1 13.6 us: per_device(): jnp.dot(normed, lax.all_gather(qkv_weight, 'fsdp', axis=0, tiled=True), p...]
    reduce_sum x2 -> x0, other arithmetic: 3.2 us -> none  [the longest x1 3.11 us: per_device(): jnp.mean(floats * floats, axis=1, keepdims=True) + EPS]
    all_to_all x4 -> x0, local copies, waits for them, and re-layouts: 2.54 us -> none  [the longest x2 1.19 us: per_device(): lax.all_to_all(slots, 'dp', split_axis=0, concat_axis=0, tiled=True)]
  transfers between devices with their start and end apart: 5 -> 0, of which waited for: 4 -> 0; matrix products, arithmetic and copies ran while one was open for 15% -> 0% of each run, Pallas kernels for 0% -> 0%
where the time goes in v2:
time: 80.4 us; the launch traced here: 80.2 us
  Pallas kernels  78.3 us (97%)
  local copies, waits for them, and re-layouts  1.87 us (2%)
    pallas_call x1, Pallas kernels, per_device(): pl.pallas_call(kernel, out_shape=jax.ShapeDtypeStruct((ROWS, COLUMNS), bf...  78.3 us
    unnamed x1, local copies, waits for them, and re-layouts  1.87 us

profile of v2, /device:TPU:1, one launch (start us, length us, event | category | flops | bytes accessed | tf_op | source)
XLA Modules:
  0.0 80.2 jit_solution(8430517128328241156)
XLA Ops:
  0.0 78.3 %shard_map.55 = bf16[256,1024]{1,0:T(8,128)(2,1)} custom-call(bf16[256,8192]{1,0:T(8,128)(2,1)} %hidden.1, f32[1,8192]{1,0:T(1,128)} %bitcast.5, bf16[2,2,4,32,1280]{4,3,2,1,0:T(8,128)(2,1)} %bitcast.4, s32[1,256]{1,0:T(1,128)} %bitcast.6, s32[1,256]{1,0:T(1,128)} %bitcast.7), custom_call_target="tpu_custom_call" | custom-call | flops 5368709120 | bytes 6291456 | tf_op jit(solution)/shard_map/pallas_call | solution.py:394
  78.4 1.9 %copy.7 = bf16[256,1024]{1,0:T(8,128)(2,1)} copy(bf16[256,1024]{1,0:T(8,128)(2,1)} %shard_map.55) | data formatting | bytes 1048576

commit v3 on v2

--- a/solution.py
+++ b/solution.py
@@ -15,6 +15,7 @@
 CHUNKS = ((1024, 256), (0, 256), (512, 256), (768, 128), (896, 128))
 RING = (256, 256)
 COLUMNS = 1024
+DIRECT = (0, 1, 3, 4)
 NEAR, FAR, LINE, LAST, TWIN, TWIN_LAST = range(6)
 
 
@@ -27,8 +28,8 @@
 
 
 def kernel(
-    hidden, gain, weight, segment, target, out,
-    wide, narrow, ring, raw, normed, total, keys, values, mask, spread, collect,
+    hidden, gain_in, weight, segment_in, target_in, out,
+    wide, narrow, ring, raw, normed, gain, segment, target, total, keys, values, mask, spread, collect,
     out_wide, in_wide, out_narrow, in_narrow, slots_out, slots_in,
     local_sem, g_send, g_recv, z_send, z_recv, a_send, a_recv, s_sem,
 ):
@@ -56,12 +57,10 @@
 
     lax.fori_loop(1, PEERS, greet, 0)
 
-    load = pltpu.make_async_copy(hidden, raw, local_sem.at[0])
-    load.start()
     ring_half, ring_part = z // 4, lax.rem(z, 4)
     ring_place = (1 - ring_half) * (y * 4 + x) + ring_half * (x * 4 + y)
     own_ring = pltpu.make_async_copy(
-        weight.at[core, ring_half, ring_part, :, pl.ds(*RING)],
+        weight.at[core, ring_half, ring_part, :, :, pl.ds(*RING)],
         ring.at[ring_half, core, ring_place, ring_part],
         local_sem.at[1],
     )
@@ -70,12 +69,21 @@
     for j, (start, width) in enumerate(CHUNKS):
         for half, (line, place) in enumerate(((y, x), (x, y))):
             copy = pltpu.make_async_copy(
-                weight.at[core, half, :, :, pl.ds(start, width)],
+                weight.at[core, half, :, :, :, pl.ds(start, width)],
                 chunk(j).at[half, core, line, place],
                 local_sem.at[2 + 2 * j + half],
             )
             copy.start()
             own.append(copy)
+
+    loads = [
+        pltpu.make_async_copy(source, landing, local_sem.at[2 + 2 * len(CHUNKS) + n])
+        for n, (source, landing) in enumerate(
+            ((target_in, target), (segment_in, segment), (gain_in, gain), (hidden, raw))
+        )
+    ]
+    for copy in loads:
+        copy.start()
 
     def send(view, device, send_sem, recv_sem):
         pltpu.make_async_remote_copy(
@@ -96,6 +104,9 @@
         send(g.at[0, core, y, x], to_x_down, s, r)
         send(g.at[1, core, x, y], to_y_up, s, r)
         send(g.at[1, core, x, y], to_y_down, s, r)
+        if j in DIRECT:
+            send(g.at[0, core, y, x], (dp, y * 4 + x_far), s, r)
+            send(g.at[1, core, x, y], (dp, y_far * 4 + x), s, r)
 
     def far(j):
         g, s, r = chunk(j), g_send.at[j], g_recv.at[j, FAR]
@@ -107,7 +118,10 @@
 
     def lines(j):
         g, s, r, t = chunk(j), g_send.at[j], g_recv.at[j, LINE], g_recv.at[j, TWIN]
-        landed(g.at[0, core, y, low], g_recv.at[j, FAR])
+        if j in DIRECT:
+            landed(g.at[0, core, pl.ds(0, 2), pl.ds(0, 3)], g_recv.at[j, NEAR])
+        else:
+            landed(g.at[0, core, y, low], g_recv.at[j, FAR])
         send(g.at[0, core, y], to_y_up, s, r)
         send(g.at[0, core, y], to_y_down, s, r)
         send(g.at[1, core, x], to_x_up, s, r)
@@ -139,11 +153,8 @@
     def twin_last(j):
         landed(chunk(j).at[:, other, 0], g_recv.at[j, TWIN_LAST])
 
-    def ring_at(where, places=None):
-        place = slice(None) if places is None else places
-        return ring.at[where // 4, core, place, lax.rem(where, 4)]
-
-    halves = (pl.ds(0, 8), pl.ds(8, 8))
+    def ring_at(where, h):
+        return ring.at[where // 4, core, :, lax.rem(where, 4), h]
 
     def z_up(n):
         return lax.rem(z + n, 8)
@@ -151,42 +162,45 @@
     def z_down(n):
         return lax.rem(z + 8 - n, 8)
 
-    def plane():
-        own_ring.wait()
-        view = ring.at[ring_half, core, ring_place, ring_part]
+    def plane(h):
+        view = ring.at[ring_half, core, ring_place, ring_part, h]
 
         def ship(k, carry):
-            send(view, (dp, lax.rem(fsdp + k, PEERS)), z_send.at[0], z_recv.at[0])
+            send(view, (dp, lax.rem(fsdp + k, PEERS)), z_send.at[0], z_recv.at[1 + h])
             return carry
 
         lax.fori_loop(1, PEERS, ship, 0)
 
-    def ring_start():
-        landed(ring_at(z, pl.ds(0, 15)), z_recv.at[0])
-        for h in range(2):
-            send(ring_at(z, halves[h]), to_z_up, z_send.at[1], z_recv.at[2 + h])
-            send(ring_at(z, halves[h]), to_z_down, z_send.at[1], z_recv.at[2 + h])
-        send(ring_at(z), sibling, z_send.at[1], z_recv.at[1])
+    def to_sibling(where, h):
+        send(ring_at(where, h), sibling, z_send.at[1], z_recv.at[0])
+
+    def ring_start(h):
+        landed(ring.at[ring_half, core, pl.ds(0, 15), ring_part, h], z_recv.at[1 + h])
+        send(ring_at(z, h), to_z_up, z_send.at[1], z_recv.at[3 + h])
+        send(ring_at(z, h), to_z_down, z_send.at[1], z_recv.at[3 + h])
+        to_sibling(z, h)
 
     def ring_step(n, h):
-        landed(ring_at(z), z_recv.at[2 * n + h])
-        sem = z_recv.at[2 * n + 2 + h]
+        landed(ring.at[ring_half, core, :, ring_part], z_recv.at[2 * n + 1 + h])
+        sem = z_recv.at[2 * n + 3 + h] if n < 3 else z_recv.at[9]
         if n < 3 or h == 0:
-            send(ring_at(z_down(n), halves[h]), to_z_up, z_send.at[1], sem if n < 3 else z_recv.at[8])
+            send(ring_at(z_down(n), h), to_z_up, z_send.at[1], sem)
         if n < 3 or h == 1:
-            send(ring_at(z_up(n), halves[h]), to_z_down, z_send.at[1], sem if n < 3 else z_recv.at[8])
-        if h == 1:
-            send(ring_at(z_down(n)), sibling, z_send.at[1], z_recv.at[1])
-            send(ring_at(z_up(n)), sibling, z_send.at[1], z_recv.at[1])
+            send(ring_at(z_up(n), h), to_z_down, z_send.at[1], sem)
+        to_sibling(z_down(n), h)
+        to_sibling(z_up(n), h)
 
     def ring_end():
-        landed(ring_at(z), z_recv.at[8])
-        send(ring_at(z_up(4)), sibling, z_send.at[1], z_recv.at[1])
+        landed(ring.at[ring_half, core, :, ring_part], z_recv.at[9])
+        to_sibling(z_up(4), 0)
+        to_sibling(z_up(4), 1)
 
     def ring_twin():
-        landed(ring.at[:, other], z_recv.at[1])
+        landed(ring.at[:, other], z_recv.at[0])
 
     def plan():
+        loads[0].wait()
+        loads[1].wait()
         goal = target[...]
         shard, slot = goal >> 12, goal & (ROWS - 1)
         chosen = lax.broadcasted_iota(jnp.int32, (PEERS, ROWS), 0) == shard
@@ -237,6 +251,9 @@
             collect[:, t * 128 : (t + 1) * 128] = (wanted == row).astype(jnp.bfloat16)
 
     def normalise():
+        loads[2].wait()
+        loads[3].wait()
+
         def some(i, carry):
             rows = pl.ds(pl.multiple_of(i * 16, 16), 16)
             floats = raw[rows, :].astype(jnp.float32)
@@ -255,44 +272,58 @@
 
         lax.fori_loop(0, ROWS // 16, some, 0)
 
-    def project(g, width):
-        total[:, :width] = jnp.zeros((ROWS, width), jnp.float32)
+    def project_ring():
+        total[5] = jnp.zeros((ROWS, 256), jnp.float32)
 
         def some(i, carry):
             columns = pl.ds(pl.multiple_of(i * 2048, 2048), 2048)
-            block = g[i // 2, lax.rem(i, 2)].reshape(2048, width)
-            total[:, :width] += nn(normed[:, columns], block)
+            block = ring[i // 2, lax.rem(i, 2)].reshape(2048, 256)
+            total[5] += nn(normed[:, columns], block)
             return carry
 
         lax.fori_loop(0, 4, some, 0)
 
-    def project_lines(j, mine, width):
-        g = chunk(j)
-        sums = jnp.zeros((ROWS, width), jnp.float32)
+    def project_lines(j, c, mine):
+        g, width = chunk(j), CHUNKS[j][1]
+        sums = None
         for half in range(2):
-            for c in range(2):
-                for line in mine[half]:
-                    first = ((half * 2 + c) * 16 + line * 4) * 128
-                    columns = pl.ds(pl.multiple_of(first, 512), 512)
-                    sums = sums + nn(normed[:, columns], g[half, c, line].reshape(512, width))
+            for line in mine[half]:
+                first = ((half * 2 + c) * 16 + line * 4) * 128
+                columns = pl.ds(pl.multiple_of(first, 512), 512)
+                part = nn(normed[:, columns], g[half, c, line].reshape(512, width))
+                sums = part if sums is None else sums + part
         return sums
 
-    def project_first(j, width):
-        total[:, :width] = project_lines(j, ((y, y_up, y_down), (x, x_up, x_down)), width)
-
-    def project_last(j, width):
-        total[:, :width] += project_lines(j, ((y_far,), (x_far,)), width)
+    near_lines, far_lines = ((y, y_up, y_down), (x, x_up, x_down)), ((y_far,), (x_far,))
+
+    def project_own(j):
+        total[j, :, : CHUNKS[j][1]] = project_lines(j, core, near_lines)
+
+    def project_twin(j):
+        twin(j)
+        total[j, :, : CHUNKS[j][1]] += project_lines(j, other, near_lines)
+
+    def project_last(j):
+        sums = project_lines(j, core, far_lines)
+        twin_last(j)
+        total[j, :, : CHUNKS[j][1]] += sums + project_lines(j, other, far_lines)
+
+    def keep():
+        keys[...] = total[0, :, :HEAD].astype(jnp.bfloat16)
+        values[...] = total[0, :, HEAD:].astype(jnp.bfloat16)
 
     def group(n):
+        if n == 5:
+            return out_wide.at[2], in_wide.at[2], 256, RING[0]
         if n < 3:
-            return out_wide.at[n], in_wide.at[n], 256, (RING[0], 0, 512)[n]
-        return out_narrow.at[n - 3], in_narrow.at[n - 3], 128, (768, 896)[n - 3]
+            return out_wide.at[n - 1], in_wide.at[n - 1], 256, CHUNKS[n][0]
+        return out_narrow.at[n - 3], in_narrow.at[n - 3], 128, CHUNKS[n][0]
 
     def attend(n):
         outgoing, incoming, width, start = group(n)
         contexts = []
         for h in range(width // HEAD):
-            query = total[:, h * HEAD : (h + 1) * HEAD].astype(jnp.bfloat16)
+            query = total[n, :, h * HEAD : (h + 1) * HEAD].astype(jnp.bfloat16)
             scores = nt(query, keys[...]) * HEAD ** (-0.5)
             scores = jnp.where(mask[...] > 0.5, scores, -1e30)
             expos = jnp.exp(scores - jnp.max(scores, axis=1, keepdims=True))
@@ -300,90 +331,87 @@
             contexts.append(nn(weights, values[...]).astype(jnp.bfloat16))
         context = jnp.concatenate(contexts, axis=1) if len(contexts) > 1 else contexts[0]
         outgoing[...] = nn(spread[...], context).astype(jnp.bfloat16).reshape(PEERS, CAPACITY, width)
-        to_peers(outgoing, incoming, a_send.at[n], a_recv.at[n])
+        to_peers(outgoing, incoming, a_send.at[n - 1], a_recv.at[n - 1])
 
     def deliver(n):
         outgoing, incoming, width, start = group(n)
-        from_peers(incoming, a_recv.at[n])
+        from_peers(incoming, a_recv.at[n - 1])
         rows = incoming[...].reshape(PEERS * CAPACITY, width)
         out[:, start : start + width] = nn(collect[...], rows).astype(jnp.bfloat16)
 
-    plan()
-    load.wait()
-    normalise()
     pl.semaphore_wait(barrier, 2 * (PEERS - 1))
-
-    plane()
     near(0)
+    own_ring.wait()
+    plane(0)
+    plane(1)
     near(1)
     near(2)
+    plan()
     to_peers(slots_out, slots_in, s_sem.at[0], s_sem.at[1])
-    ring_start()
-    far(0)
+    normalise()
+    lines(0)
+    ring_start(0)
+    ring_start(1)
+    lines(1)
+    far(2)
+    ring_step(1, 0)
+    ring_step(1, 1)
+    plan_arrivals()
+    pass_lines(0)
+    project_own(0)
+    ring_step(2, 0)
+    project_twin(0)
+    pass_lines(1)
+    lines(2)
     near(3)
     near(4)
-    far(1)
-    far(2)
-    lines(0)
-    far(3)
-    far(4)
-    ring_step(1, 0)
-    lines(1)
-    ring_step(1, 1)
-    plan_arrivals()
-    ring_step(2, 0)
-    pass_lines(0)
-    lines(2)
     ring_step(2, 1)
+    project_own(1)
+    last_lines(0)
+    project_last(0)
+    keep()
     ring_step(3, 0)
-    pass_lines(1)
+    project_twin(1)
     ring_step(3, 1)
-    last_lines(0)
+    last_lines(1)
+    project_last(1)
+    attend(1)
+    ring_end()
+    pass_lines(2)
     lines(3)
-    twin(0)
-    twin_last(0)
-    project(chunk(0), 256)
-    keys[...] = total[:, :HEAD].astype(jnp.bfloat16)
-    values[...] = total[:, HEAD:].astype(jnp.bfloat16)
-    ring_end()
+    lines(4)
     ring_twin()
-    project(ring, 256)
-    pass_lines(2)
-    lines(4)
-    attend(0)
-    last_lines(1)
-    twin(1)
-    twin_last(1)
-    project(chunk(1), 256)
+    project_ring()
+    attend(5)
+    project_own(2)
+    project_twin(2)
+    last_lines(2)
     pass_lines(3)
-    attend(1)
-    last_lines(2)
-    twin(2)
-    twin_last(2)
-    project(chunk(2), 256)
+    project_last(2)
+    attend(2)
+    project_own(3)
     pass_lines(4)
-    attend(2)
-    twin(3)
-    project_first(3, 128)
+    project_twin(3)
     last_lines(3)
-    twin_last(3)
-    project_last(3, 128)
+    project_last(3)
     attend(3)
-    twin(4)
-    project_first(4, 128)
+    project_own(4)
+    project_twin(4)
     last_lines(4)
-    twin_last(4)
-    project_last(4, 128)
+    project_last(4)
     attend(4)
-    for n in range(5):
-        deliver(n)
+    deliver(1)
+    deliver(5)
+    deliver(2)
+    deliver(3)
+    deliver(4)
     for j, (start, width) in enumerate(CHUNKS):
         landed(raw.at[pl.ds(0, width), pl.ds(0, 7936)], g_send.at[j])
     landed(raw.at[pl.ds(0, 16), pl.ds(0, 7680)], z_send.at[0])
     landed(raw.at[pl.ds(0, 240)], z_send.at[1])
     landed(slots_out.at[pl.ds(0, PEERS - 1)], s_sem.at[0])
-    for n in range(5):
-        landed(group(n)[0].at[pl.ds(0, PEERS - 1)], a_send.at[n])
+    for n in range(1, 6):
+        landed(group(n)[0].at[pl.ds(0, PEERS - 1)], a_send.at[n - 1])
 
 
 def per_device(hidden, gain, qkv_weight, owner_segment, target_row):
@@ -393,16 +421,19 @@
     dma = pltpu.SemaphoreType.DMA
     return pl.pallas_call(
         kernel,
-        out_shape=jax.ShapeDtypeStruct((ROWS, COLUMNS), bf16),
-        in_specs=[any_space, vmem, any_space, vmem, vmem],
+        out_shape=pltpu.VMEM((ROWS, COLUMNS), bf16),
+        in_specs=[any_space] * 5,
         out_specs=vmem,
         scratch_shapes=[
-            pltpu.VMEM((3, 2, 2, 4, 4, 4, 32, 256), bf16),
-            pltpu.VMEM((2, 2, 2, 4, 4, 4, 32, 128), bf16),
-            pltpu.VMEM((2, 2, 16, 4, 32, 256), bf16),
+            pltpu.VMEM((3, 2, 2, 4, 4, 4, 2, 16, 256), bf16),
+            pltpu.VMEM((2, 2, 2, 4, 4, 4, 2, 16, 128), bf16),
+            pltpu.VMEM((2, 2, 16, 4, 2, 16, 256), bf16),
             pltpu.VMEM((ROWS, FEATURES), bf16),
             pltpu.VMEM((ROWS, FEATURES), bf16),
-            pltpu.VMEM((ROWS, 256), f32),
+            pltpu.VMEM((1, FEATURES), f32),
+            pltpu.VMEM((1, ROWS), jnp.int32),
+            pltpu.VMEM((1, ROWS), jnp.int32),
+            pltpu.VMEM((6, ROWS, 256), f32),
             pltpu.VMEM((ROWS, HEAD), bf16),
             pltpu.VMEM((ROWS, HEAD), bf16),
             pltpu.VMEM((ROWS, ROWS), f32),
@@ -414,11 +445,11 @@
             pltpu.VMEM((2, PEERS, CAPACITY, 128), bf16),
             pltpu.VMEM((PEERS, 8, 128), f32),
             pltpu.VMEM((PEERS, 8, 128), f32),
-            dma((2 + 2 * len(CHUNKS),)),
+            dma((6 + 2 * len(CHUNKS),)),
             dma((len(CHUNKS),)),
             dma((len(CHUNKS), 6)),
             dma((2,)),
-            dma((9,)),
+            dma((10,)),
             dma((5,)),
             dma((5,)),
             dma((2,)),
@@ -432,7 +463,7 @@
     )(
         hidden,
         gain.reshape(1, FEATURES),
-        qkv_weight.reshape(2, 2, 4, 32, 1280),
+        qkv_weight.reshape(2, 2, 4, 2, 16, 1280),
         owner_segment.reshape(1, ROWS),
         target_row.reshape(1, ROWS),
     )

time: 80.4 us -> 74.6 us (0.928)
  Pallas kernels: 78.3 us -> 73.7 us
  local copies, waits for them, and re-layouts: 1.87 us -> 0.8 us
    pallas_call x1, Pallas kernels: 78.3 us -> 73.7 us  [per_device(): pl.pallas_call(kernel, out_shape=pltpu.VMEM((ROWS, COLUMNS), bf16), in_sp...]
    unnamed x1, local copies, waits for them, and re-layouts: 1.87 us -> 0.8 us
where the time goes in v3:
time: 74.6 us; the launch traced here: 74.5 us
  Pallas kernels  73.7 us (99%)
  local copies, waits for them, and re-layouts  0.8 us (1%)
    pallas_call x1, Pallas kernels, per_device(): pl.pallas_call(kernel, out_shape=pltpu.VMEM((ROWS, COLUMNS), bf16), in_sp...  73.7 us

profile of v3, /device:TPU:1, one launch (start us, length us, event | category | flops | bytes accessed | tf_op | source)
XLA Modules:
  0.0 74.5 jit_solution(757281824581156234)
XLA Ops:
  0.0 73.7 %shard_map.55 = bf16[256,1024]{1,0:T(8,128)(2,1)S(1)} custom-call(bf16[256,8192]{1,0:T(8,128)(2,1)} %hidden.1, f32[1,8192]{1,0:T(1,128)} %bitcast.5, bf16[2,2,4,2,16,1280]{5,4,3,2,1,0:T(8,128)(2,1)} %bitcast.4, s32[1,256]{1,0:T(1,128)} %bitcast.6, s32[1,256]{1,0:T(1,128)} %bitcast.7), custom_call_target="tpu_custom_call" | custom-call | flops 5368709120 | bytes 6291456 | tf_op jit(solution)/shard_map/pallas_call | solution.py:422
  73.7 0.8 %copy.7 = bf16[256,1024]{1,0:T(8,128)(2,1)} copy(bf16[256,1024]{1,0:T(8,128)(2,1)S(1)} %shard_map.55) | data formatting | bytes 1048576

commit v4 on v3

--- a/solution.py
+++ b/solution.py
@@ -31,7 +31,7 @@
     hidden, gain_in, weight, segment_in, target_in, out,
     wide, narrow, ring, raw, normed, gain, segment, target, total, keys, values, mask, spread, collect,
     out_wide, in_wide, out_narrow, in_narrow, slots_out, slots_in,
-    local_sem, g_send, g_recv, z_send, z_recv, a_send, a_recv, s_sem,
+    local_sem, g_send, g_recv, z_send, z_recv, a_send, a_recv, s_sem, word,
 ):
     dp, fsdp = lax.axis_index("dp"), lax.axis_index("fsdp")
     z, core = dp // 2, lax.rem(dp, 2)
@@ -44,24 +44,30 @@
     to_z_up = (lax.rem(z + 1, 8) * 2 + core, fsdp)
     to_z_down = (lax.rem(z + 7, 8) * 2 + core, fsdp)
     sibling = (dp + other - core, fsdp)
+    to_x_far, to_y_far = (dp, y * 4 + x_far), (dp, y_far * 4 + x)
 
     def chunk(j):
         return wide.at[j] if j < 3 else narrow.at[j - 3]
 
     barrier = pltpu.get_barrier_semaphore()
 
-    def greet(k, carry):
-        for peer in ((lax.rem(dp + k, PEERS), fsdp), (dp, lax.rem(fsdp + k, PEERS))):
-            pl.semaphore_signal(barrier, inc=1, device_id=peer, device_id_type=MESH)
-        return carry
-
-    lax.fori_loop(1, PEERS, greet, 0)
+    for peer in (
+        to_x_up, to_x_down, to_y_up, to_y_down, to_x_far, to_y_far, to_z_up, to_z_down, sibling
+    ):
+        pl.semaphore_signal(barrier, inc=1, device_id=peer, device_id_type=MESH)
+
+    def tell(n):
+        for peer in (to_z_up, to_z_down):
+            pl.semaphore_signal(word.at[n], inc=1, device_id=peer, device_id_type=MESH)
+
+    def hear(n):
+        pl.semaphore_wait(word.at[n], 2)
 
     ring_half, ring_part = z // 4, lax.rem(z, 4)
-    ring_place = (1 - ring_half) * (y * 4 + x) + ring_half * (x * 4 + y)
+    u, v = (1 - ring_half) * y + ring_half * x, (1 - ring_half) * x + ring_half * y
     own_ring = pltpu.make_async_copy(
         weight.at[core, ring_half, ring_part, :, :, pl.ds(*RING)],
-        ring.at[ring_half, core, ring_place, ring_part],
+        ring.at[ring_half, core, u, v, ring_part],
         local_sem.at[1],
     )
     own_ring.start()
@@ -154,7 +160,7 @@
         landed(chunk(j).at[:, other, 0], g_recv.at[j, TWIN_LAST])
 
     def ring_at(where, h):
-        return ring.at[where // 4, core, :, lax.rem(where, 4), h]
+        return ring.at[where // 4, core, :, :, lax.rem(where, 4), h]
 
     def z_up(n):
         return lax.rem(z + n, 8)
@@ -162,26 +168,36 @@
     def z_down(n):
         return lax.rem(z + 8 - n, 8)
 
+    def beside(k, along):
+        u_to, v_to = lax.rem(u + k * (1 - along), 4), lax.rem(v + k * along, 4)
+        return (dp, (1 - ring_half) * (u_to * 4 + v_to) + ring_half * (v_to * 4 + u_to))
+
     def plane(h):
-        view = ring.at[ring_half, core, ring_place, ring_part, h]
-
-        def ship(k, carry):
-            send(view, (dp, lax.rem(fsdp + k, PEERS)), z_send.at[0], z_recv.at[1 + h])
-            return carry
-
-        lax.fori_loop(1, PEERS, ship, 0)
+        for k in (1, 3, 2):
+            view = ring.at[ring_half, core, u, v, ring_part, h]
+            send(view, beside(k, 1 - h), z_send.at[0], z_recv.at[10 + h])
+
+    def plane_lines(h):
+        view = ring.at[ring_half, core, u, pl.ds(0, 3), ring_part, h]
+        landed(view, z_recv.at[10 + h])
+        if h == 0:
+            view = ring.at[ring_half, core, u, :, ring_part, h]
+        else:
+            view = ring.at[ring_half, core, :, v, ring_part, h]
+        for k in (1, 3, 2):
+            send(view, beside(k, h), z_send.at[0], z_recv.at[1 + h])
 
     def to_sibling(where, h):
         send(ring_at(where, h), sibling, z_send.at[1], z_recv.at[0])
 
     def ring_start(h):
-        landed(ring.at[ring_half, core, pl.ds(0, 15), ring_part, h], z_recv.at[1 + h])
+        landed(ring.at[ring_half, core, pl.ds(0, 3), :, ring_part, h], z_recv.at[1 + h])
         send(ring_at(z, h), to_z_up, z_send.at[1], z_recv.at[3 + h])
         send(ring_at(z, h), to_z_down, z_send.at[1], z_recv.at[3 + h])
         to_sibling(z, h)
 
     def ring_step(n, h):
-        landed(ring.at[ring_half, core, :, ring_part], z_recv.at[2 * n + 1 + h])
+        landed(ring.at[ring_half, core, :, :, ring_part], z_recv.at[2 * n + 1 + h])
         sem = z_recv.at[2 * n + 3 + h] if n < 3 else z_recv.at[9]
         if n < 3 or h == 0:
             send(ring_at(z_down(n), h), to_z_up, z_send.at[1], sem)
@@ -191,7 +207,7 @@
         to_sibling(z_up(n), h)
 
     def ring_end():
-        landed(ring.at[ring_half, core, :, ring_part], z_recv.at[9])
+        landed(ring.at[ring_half, core, :, :, ring_part], z_recv.at[9])
         to_sibling(z_up(4), 0)
         to_sibling(z_up(4), 1)
 
@@ -250,9 +266,10 @@
             row = row[0:1].astype(jnp.int32)
             collect[:, t * 128 : (t + 1) * 128] = (wanted == row).astype(jnp.bfloat16)
 
-    def normalise():
-        loads[2].wait()
-        loads[3].wait()
+    def normalise(part):
+        if part == 0:
+            loads[2].wait()
+            loads[3].wait()
 
         def some(i, carry):
             rows = pl.ds(pl.multiple_of(i * 16, 16), 16)
@@ -270,7 +287,7 @@
                         )
             return carry
 
-        lax.fori_loop(0, ROWS // 16, some, 0)
+        lax.fori_loop(part * 8, part * 8 + 8, some, 0)
 
     def project_ring():
         total[5] = jnp.zeros((ROWS, 256), jnp.float32)
@@ -339,34 +356,44 @@
         rows = incoming[...].reshape(PEERS * CAPACITY, width)
         out[:, start : start + width] = nn(collect[...], rows).astype(jnp.bfloat16)
 
-    pl.semaphore_wait(barrier, 2 * (PEERS - 1))
-    near(0)
+    pl.semaphore_wait(barrier, 9)
+    tell(0)
     own_ring.wait()
     plane(0)
     plane(1)
+    near(0)
     near(1)
+    plan()
+    normalise(0)
+    plane_lines(0)
+    plane_lines(1)
     near(2)
-    plan()
-    to_peers(slots_out, slots_in, s_sem.at[0], s_sem.at[1])
-    normalise()
+    normalise(1)
     lines(0)
+    hear(0)
+    tell(1)
+    lines(1)
     ring_start(0)
     ring_start(1)
-    lines(1)
     far(2)
+    hear(1)
+    tell(2)
     ring_step(1, 0)
+    pass_lines(0)
     ring_step(1, 1)
-    plan_arrivals()
-    pass_lines(0)
     project_own(0)
+    hear(2)
+    tell(3)
+    project_twin(0)
     ring_step(2, 0)
-    project_twin(0)
     pass_lines(1)
     lines(2)
     near(3)
     near(4)
     ring_step(2, 1)
     project_own(1)
+    hear(3)
+    to_peers(slots_out, slots_in, s_sem.at[0], s_sem.at[1])
     last_lines(0)
     project_last(0)
     keep()
@@ -377,6 +404,7 @@
     project_last(1)
     attend(1)
     ring_end()
+    plan_arrivals()
     pass_lines(2)
     lines(3)
     lines(4)
@@ -427,7 +455,7 @@
         scratch_shapes=[
             pltpu.VMEM((3, 2, 2, 4, 4, 4, 2, 16, 256), bf16),
             pltpu.VMEM((2, 2, 2, 4, 4, 4, 2, 16, 128), bf16),
-            pltpu.VMEM((2, 2, 16, 4, 2, 16, 256), bf16),
+            pltpu.VMEM((2, 2, 4, 4, 4, 2, 16, 256), bf16),
             pltpu.VMEM((ROWS, FEATURES), bf16),
             pltpu.VMEM((ROWS, FEATURES), bf16),
             pltpu.VMEM((1, FEATURES), f32),
@@ -449,10 +477,11 @@
             dma((len(CHUNKS),)),
             dma((len(CHUNKS), 6)),
             dma((2,)),
-            dma((10,)),
+            dma((12,)),
             dma((5,)),
             dma((5,)),
             dma((2,)),
+            pltpu.SemaphoreType.REGULAR((4,)),
         ],
         compiler_params=pltpu.CompilerParams(
             collective_id=0, has_side_effects=True, vmem_limit_bytes=56 << 20

time: 74.6 us -> 72.8 us (0.976)
  Pallas kernels: 73.7 us -> 72 us
    pallas_call x1, Pallas kernels: 73.7 us -> 72 us  [per_device(): pl.pallas_call(kernel, out_shape=pltpu.VMEM((ROWS, COLUMNS), bf16), in_sp...]
where the time goes in v4:
time: 72.8 us
  Pallas kernels  72 us (99%)
  local copies, waits for them, and re-layouts  0.8 us (1%)
    pallas_call x1, Pallas kernels, per_device(): pl.pallas_call(kernel, out_shape=pltpu.VMEM((ROWS, COLUMNS), bf16), in_sp...  72 us

profile of v4, /device:TPU:1, one launch (start us, length us, event | category | flops | bytes accessed | tf_op | source)
XLA Modules:
  0.0 72.8 jit_solution(7092702217844413585)
XLA Ops:
  0.0 72.0 %shard_map.55 = bf16[256,1024]{1,0:T(8,128)(2,1)S(1)} custom-call(bf16[256,8192]{1,0:T(8,128)(2,1)} %hidden.1, f32[1,8192]{1,0:T(1,128)} %bitcast.5, bf16[2,2,4,2,16,1280]{5,4,3,2,1,0:T(8,128)(2,1)} %bitcast.4, s32[1,256]{1,0:T(1,128)} %bitcast.6, s32[1,256]{1,0:T(1,128)} %bitcast.7), custom_call_target="tpu_custom_call" | custom-call | flops 5368709120 | bytes 6291456 | tf_op jit(solution)/shard_map/pallas_call | solution.py:450
  72.0 0.8 %copy.7 = bf16[256,1024]{1,0:T(8,128)(2,1)} copy(bf16[256,1024]{1,0:T(8,128)(2,1)S(1)} %shard_map.55) | data formatting | bytes 1048576

commit v5 on v4

--- a/solution.py
+++ b/solution.py
@@ -1,3 +1,5 @@
+import math
+
 import jax
 import jax.numpy as jnp
 from jax import lax
@@ -8,6 +10,7 @@
 MESH = pl.DeviceIdType.MESH
 HEAD = 128
 EPS = 1e-05
+SCALE = HEAD ** (-0.5) * math.log2(math.e)
 ROWS = 256
 FEATURES = 8192
 PEERS = 16
@@ -68,24 +71,24 @@
     own_ring = pltpu.make_async_copy(
         weight.at[core, ring_half, ring_part, :, :, pl.ds(*RING)],
         ring.at[ring_half, core, u, v, ring_part],
-        local_sem.at[1],
+        local_sem.at[2],
     )
     own_ring.start()
-    own = []
     for j, (start, width) in enumerate(CHUNKS):
         for half, (line, place) in enumerate(((y, x), (x, y))):
-            copy = pltpu.make_async_copy(
+            pltpu.make_async_copy(
                 weight.at[core, half, :, :, :, pl.ds(start, width)],
                 chunk(j).at[half, core, line, place],
-                local_sem.at[2 + 2 * j + half],
-            )
-            copy.start()
-            own.append(copy)
+                local_sem.at[3],
+            ).start()
 
     loads = [
-        pltpu.make_async_copy(source, landing, local_sem.at[2 + 2 * len(CHUNKS) + n])
-        for n, (source, landing) in enumerate(
-            ((target_in, target), (segment_in, segment), (gain_in, gain), (hidden, raw))
+        pltpu.make_async_copy(source, landing, sem)
+        for source, landing, sem in (
+            (target_in, target, local_sem.at[0]),
+            (segment_in, segment, local_sem.at[1]),
+            (gain_in, gain, local_sem.at[4]),
+            (hidden, raw, local_sem.at[5]),
         )
     ]
     for copy in loads:
@@ -102,10 +105,12 @@
 
     low, high = pl.ds(0, 2), pl.ds(2, 2)
 
+    def own_blocks():
+        own_ring.wait()
+        landed(raw.at[pl.ds(0, 32), pl.ds(0, FEATURES)], local_sem.at[3])
+
     def near(j):
         g, s, r = chunk(j), g_send.at[j], g_recv.at[j, NEAR]
-        own[2 * j].wait()
-        own[2 * j + 1].wait()
         send(g.at[0, core, y, x], to_x_up, s, r)
         send(g.at[0, core, y, x], to_x_down, s, r)
         send(g.at[1, core, x, y], to_y_up, s, r)
@@ -240,11 +245,11 @@
         causal = lax.broadcasted_iota(jnp.int32, (ROWS, ROWS), 1) <= lax.broadcasted_iota(
             jnp.int32, (ROWS, ROWS), 0
         )
-        mask[...] = ((ids == ids.T) & causal).astype(jnp.float32)
+        mask[...] = jnp.where((ids == ids.T) & causal, 0.0, -1e30)
 
     def to_peers(source, landing, send_sem, recv_sem):
         def ship(k, carry):
-            peer = lax.rem(dp + k, PEERS)
+            peer = lax.rem(dp + 8 + (k + 1) // 2 * (1 - 2 * lax.rem(k, 2)), PEERS)
             pltpu.make_async_remote_copy(
                 src_ref=source.at[peer], dst_ref=landing.at[dp],
                 send_sem=send_sem, recv_sem=recv_sem,
@@ -252,7 +257,7 @@
             ).start()
             return carry
 
-        lax.fori_loop(1, PEERS, ship, 0)
+        lax.fori_loop(0, PEERS - 1, ship, 0)
         landing[dp] = source[dp]
 
     def from_peers(landing, recv_sem):
@@ -341,14 +346,13 @@
         contexts = []
         for h in range(width // HEAD):
             query = total[n, :, h * HEAD : (h + 1) * HEAD].astype(jnp.bfloat16)
-            scores = nt(query, keys[...]) * HEAD ** (-0.5)
-            scores = jnp.where(mask[...] > 0.5, scores, -1e30)
-            expos = jnp.exp(scores - jnp.max(scores, axis=1, keepdims=True))
-            weights = (expos / jnp.sum(expos, axis=1, keepdims=True)).astype(jnp.bfloat16)
+            scores = nt(query, keys[...]) + mask[...]
+            expos = jnp.exp2((scores - jnp.max(scores, axis=1, keepdims=True)) * SCALE)
+            weights = (expos * (1.0 / jnp.sum(expos, axis=1, keepdims=True))).astype(jnp.bfloat16)
             contexts.append(nn(weights, values[...]).astype(jnp.bfloat16))
         context = jnp.concatenate(contexts, axis=1) if len(contexts) > 1 else contexts[0]
         outgoing[...] = nn(spread[...], context).astype(jnp.bfloat16).reshape(PEERS, CAPACITY, width)
-        to_peers(outgoing, incoming, a_send.at[n - 1], a_recv.at[n - 1])
+        to_peers(outgoing, incoming, a_send.at[0], a_recv.at[n - 1])
 
     def deliver(n):
         outgoing, incoming, width, start = group(n)
@@ -358,7 +362,7 @@
 
     pl.semaphore_wait(barrier, 9)
     tell(0)
-    own_ring.wait()
+    own_blocks()
     plane(0)
     plane(1)
     near(0)
@@ -406,10 +410,10 @@
     ring_end()
     plan_arrivals()
     pass_lines(2)
+    ring_twin()
+    project_ring()
     lines(3)
     lines(4)
-    ring_twin()
-    project_ring()
     attend(5)
     project_own(2)
     project_twin(2)
@@ -438,9 +442,7 @@
     landed(raw.at[pl.ds(0, 16), pl.ds(0, 7680)], z_send.at[0])
     landed(raw.at[pl.ds(0, 240)], z_send.at[1])
     landed(slots_out.at[pl.ds(0, PEERS - 1)], s_sem.at[0])
-    for n in range(1, 6):
-        landed(group(n)[0].at[pl.ds(0, PEERS - 1)], a_send.at[n - 1])
-
+    landed(raw.at[pl.ds(0, 64), pl.ds(0, 7680)], a_send.at[0])
 
 def per_device(hidden, gain, qkv_weight, owner_segment, target_row):
     any_space = pl.BlockSpec(memory_space=pl.ANY)
@@ -473,12 +475,12 @@
             pltpu.VMEM((2, PEERS, CAPACITY, 128), bf16),
             pltpu.VMEM((PEERS, 8, 128), f32),
             pltpu.VMEM((PEERS, 8, 128), f32),
-            dma((6 + 2 * len(CHUNKS),)),
+            dma((6,)),
             dma((len(CHUNKS),)),
             dma((len(CHUNKS), 6)),
             dma((2,)),
             dma((12,)),
-            dma((5,)),
+            dma((1,)),
             dma((5,)),
             dma((2,)),
             pltpu.SemaphoreType.REGULAR((4,)),

time: 72.8 us -> 71 us (0.975)
  Pallas kernels: 72 us -> 70.1 us
    pallas_call x1, Pallas kernels: 72 us -> 70.1 us  [per_device(): pl.pallas_call(kernel, out_shape=pltpu.VMEM((ROWS, COLUMNS), bf16), in_sp...]
where the time goes in v5:
time: 71 us; the launch traced here: 70.9 us
  Pallas kernels  70.1 us (99%)
  local copies, waits for them, and re-layouts  0.8 us (1%)
    pallas_call x1, Pallas kernels, per_device(): pl.pallas_call(kernel, out_shape=pltpu.VMEM((ROWS, COLUMNS), bf16), in_sp...  70.1 us

profile of v5, /device:TPU:1, one launch (start us, length us, event | category | flops | bytes accessed | tf_op | source)
XLA Modules:
  0.0 70.9 jit_solution(4443312676787595464)
XLA Ops:
  0.0 70.1 %shard_map.55 = bf16[256,1024]{1,0:T(8,128)(2,1)S(1)} custom-call(bf16[256,8192]{1,0:T(8,128)(2,1)} %hidden.1, f32[1,8192]{1,0:T(1,128)} %bitcast.5, bf16[2,2,4,2,16,1280]{5,4,3,2,1,0:T(8,128)(2,1)} %bitcast.4, s32[1,256]{1,0:T(1,128)} %bitcast.6, s32[1,256]{1,0:T(1,128)} %bitcast.7), custom_call_target="tpu_custom_call" | custom-call | flops 5368709120 | bytes 6291456 | tf_op jit(solution)/shard_map/pallas_call | solution.py:452
  70.1 0.8 %copy.7 = bf16[256,1024]{1,0:T(8,128)(2,1)} copy(bf16[256,1024]{1,0:T(8,128)(2,1)S(1)} %shard_map.55) | data formatting | bytes 1048576

commit v6 on v5

--- a/solution.py
+++ b/solution.py
@@ -1,5 +1,3 @@
-import math
-
 import jax
 import jax.numpy as jnp
 from jax import lax
@@ -10,7 +8,6 @@
 MESH = pl.DeviceIdType.MESH
 HEAD = 128
 EPS = 1e-05
-SCALE = HEAD ** (-0.5) * math.log2(math.e)
 ROWS = 256
 FEATURES = 8192
 PEERS = 16
@@ -54,10 +51,25 @@
 
     barrier = pltpu.get_barrier_semaphore()
 
-    for peer in (
-        to_x_up, to_x_down, to_y_up, to_y_down, to_x_far, to_y_far, to_z_up, to_z_down, sibling
-    ):
+    def here(peer):
         pl.semaphore_signal(barrier, inc=1, device_id=peer, device_id_type=MESH)
+
+    for peer in (to_x_up, to_x_down, to_y_up, to_y_down, to_x_far, to_y_far, sibling):
+        here(peer)
+    pl.when(z < 7)(lambda: here(to_z_up))
+    pl.when(z == 0)(lambda: here(to_z_down))
+
+    def entry():
+        pl.semaphore_wait(barrier, 7 + (z + 7) // 8 + z // 7)
+
+        def answer(peer):
+            pl.semaphore_signal(word.at[4], inc=1, device_id=peer, device_id_type=MESH)
+
+        pl.when(z > 0)(lambda: answer(to_z_down))
+        pl.when(z == 7)(lambda: answer(to_z_up))
+
+    def answers():
+        pl.when(z < 7)(lambda: pl.semaphore_wait(word.at[4], 2 - (z + 7) // 8))
 
     def tell(n):
         for peer in (to_z_up, to_z_down):
@@ -245,19 +257,23 @@
         causal = lax.broadcasted_iota(jnp.int32, (ROWS, ROWS), 1) <= lax.broadcasted_iota(
             jnp.int32, (ROWS, ROWS), 0
         )
-        mask[...] = jnp.where((ids == ids.T) & causal, 0.0, -1e30)
+        mask[...] = ((ids == ids.T) & causal).astype(jnp.float32)
 
     def to_peers(source, landing, send_sem, recv_sem):
-        def ship(k, carry):
-            peer = lax.rem(dp + 8 + (k + 1) // 2 * (1 - 2 * lax.rem(k, 2)), PEERS)
+        def ship(peer):
             pltpu.make_async_remote_copy(
                 src_ref=source.at[peer], dst_ref=landing.at[dp],
                 send_sem=send_sem, recv_sem=recv_sem,
                 device_id=(peer, fsdp), device_id_type=MESH,
             ).start()
+
+        def ship_two(k, carry):
+            ship(lax.rem(dp + 8 + k, PEERS))
+            ship(lax.rem(dp + 8 - k, PEERS))
             return carry
 
-        lax.fori_loop(0, PEERS - 1, ship, 0)
+        ship(lax.rem(dp + 8, PEERS))
+        lax.fori_loop(1, 8, ship_two, 0)
         landing[dp] = source[dp]
 
     def from_peers(landing, recv_sem):
@@ -346,8 +362,9 @@
         contexts = []
         for h in range(width // HEAD):
             query = total[n, :, h * HEAD : (h + 1) * HEAD].astype(jnp.bfloat16)
-            scores = nt(query, keys[...]) + mask[...]
-            expos = jnp.exp2((scores - jnp.max(scores, axis=1, keepdims=True)) * SCALE)
+            scores = nt(query, keys[...]) * HEAD ** (-0.5)
+            scores = jnp.where(mask[...] > 0.5, scores, -1e30)
+            expos = jnp.exp(scores - jnp.max(scores, axis=1, keepdims=True))
             weights = (expos * (1.0 / jnp.sum(expos, axis=1, keepdims=True))).astype(jnp.bfloat16)
             contexts.append(nn(weights, values[...]).astype(jnp.bfloat16))
         context = jnp.concatenate(contexts, axis=1) if len(contexts) > 1 else contexts[0]
@@ -360,8 +377,7 @@
         rows = incoming[...].reshape(PEERS * CAPACITY, width)
         out[:, start : start + width] = nn(collect[...], rows).astype(jnp.bfloat16)
 
-    pl.semaphore_wait(barrier, 9)
-    tell(0)
+    entry()
     own_blocks()
     plane(0)
     plane(1)
@@ -374,20 +390,20 @@
     near(2)
     normalise(1)
     lines(0)
-    hear(0)
-    tell(1)
+    answers()
+    tell(0)
     lines(1)
     ring_start(0)
     ring_start(1)
     far(2)
-    hear(1)
-    tell(2)
+    hear(0)
+    tell(1)
     ring_step(1, 0)
     pass_lines(0)
     ring_step(1, 1)
     project_own(0)
-    hear(2)
-    tell(3)
+    hear(1)
+    tell(2)
     project_twin(0)
     ring_step(2, 0)
     pass_lines(1)
@@ -396,8 +412,8 @@
     near(4)
     ring_step(2, 1)
     project_own(1)
-    hear(3)
-    to_peers(slots_out, slots_in, s_sem.at[0], s_sem.at[1])
+    hear(2)
+    tell(3)
     last_lines(0)
     project_last(0)
     keep()
@@ -406,15 +422,17 @@
     ring_step(3, 1)
     last_lines(1)
     project_last(1)
+    hear(3)
+    to_peers(slots_out, slots_in, s_sem.at[0], s_sem.at[1])
     attend(1)
     ring_end()
-    plan_arrivals()
     pass_lines(2)
     ring_twin()
     project_ring()
     lines(3)
     lines(4)
     attend(5)
+    plan_arrivals()
     project_own(2)
     project_twin(2)
     last_lines(2)
@@ -425,10 +443,10 @@
     pass_lines(4)
     project_twin(3)
     last_lines(3)
+    project_own(4)
+    project_twin(4)
     project_last(3)
     attend(3)
-    project_own(4)
-    project_twin(4)
     last_lines(4)
     project_last(4)
     attend(4)
@@ -483,7 +501,7 @@
             dma((1,)),
             dma((5,)),
             dma((2,)),
-            pltpu.SemaphoreType.REGULAR((4,)),
+            pltpu.SemaphoreType.REGULAR((5,)),
         ],
         compiler_params=pltpu.CompilerParams(
             collective_id=0, has_side_effects=True, vmem_limit_bytes=56 << 20

time: 71 us -> 70 us (0.986)
  Pallas kernels: 70.1 us -> 69.1 us
    pallas_call x1, Pallas kernels: 70.1 us -> 69.1 us  [per_device(): pl.pallas_call(kernel, out_shape=pltpu.VMEM((ROWS, COLUMNS), bf16), in_sp...]
where the time goes in v6:
time: 70 us; the launch traced here: 69.9 us
  Pallas kernels  69.1 us (99%)
  local copies, waits for them, and re-layouts  0.8 us (1%)
    pallas_call x1, Pallas kernels, per_device(): pl.pallas_call(kernel, out_shape=pltpu.VMEM((ROWS, COLUMNS), bf16), in_sp...  69.1 us

profile of v6, /device:TPU:1, one launch (start us, length us, event | category | flops | bytes accessed | tf_op | source)
XLA Modules:
  0.0 69.9 jit_solution(18308438439776410100)
XLA Ops:
  0.0 69.1 %shard_map.55 = bf16[256,1024]{1,0:T(8,128)(2,1)S(1)} custom-call(bf16[256,8192]{1,0:T(8,128)(2,1)} %hidden.1, f32[1,8192]{1,0:T(1,128)} %bitcast.5, bf16[2,2,4,2,16,1280]{5,4,3,2,1,0:T(8,128)(2,1)} %bitcast.4, s32[1,256]{1,0:T(1,128)} %bitcast.6, s32[1,256]{1,0:T(1,128)} %bitcast.7), custom_call_target="tpu_custom_call" | custom-call | flops 5368709120 | bytes 6291456 | tf_op jit(solution)/shard_map/pallas_call | solution.py:470
  69.1 0.8 %copy.7 = bf16[256,1024]{1,0:T(8,128)(2,1)} copy(bf16[256,1024]{1,0:T(8,128)(2,1)S(1)} %shard_map.55) | data formatting | bytes 1048576

commit v7 on v6

--- a/solution.py
+++ b/solution.py
@@ -428,8 +428,8 @@
     ring_end()
     pass_lines(2)
     ring_twin()
+    lines(3)
     project_ring()
-    lines(3)
     lines(4)
     attend(5)
     plan_arrivals()

time: 70 us -> 70.1 us (level)
  no operation moved by 1% of the time
where the time goes in v7:
time: 70.1 us; the launch traced here: 70 us
  Pallas kernels  69.2 us (99%)
  local copies, waits for them, and re-layouts  0.8 us (1%)
    pallas_call x1, Pallas kernels, per_device(): pl.pallas_call(kernel, out_shape=pltpu.VMEM((ROWS, COLUMNS), bf16), in_sp...  69.2 us

profile of v7, /device:TPU:1, one launch (start us, length us, event | category | flops | bytes accessed | tf_op | source)
XLA Modules:
  0.0 70.0 jit_solution(7370005117497229896)
XLA Ops:
  0.0 69.2 %shard_map.55 = bf16[256,1024]{1,0:T(8,128)(2,1)S(1)} custom-call(bf16[256,8192]{1,0:T(8,128)(2,1)} %hidden.1, f32[1,8192]{1,0:T(1,128)} %bitcast.5, bf16[2,2,4,2,16,1280]{5,4,3,2,1,0:T(8,128)(2,1)} %bitcast.4, s32[1,256]{1,0:T(1,128)} %bitcast.6, s32[1,256]{1,0:T(1,128)} %bitcast.7), custom_call_target="tpu_custom_call" | custom-call | flops 5368709120 | bytes 6291456 | tf_op jit(solution)/shard_map/pallas_call | solution.py:470
  69.2 0.8 %copy.7 = bf16[256,1024]{1,0:T(8,128)(2,1)} copy(bf16[256,1024]{1,0:T(8,128)(2,1)S(1)} %shard_map.55) | data formatting | bytes 1048576
